TPU v7x, 256 devices: a whole 4x4x8 slice. The times are simulated.
256 devices in a mesh: grp: 4 (over y), slab: 64 (over z, x, core).
Axes of the slice: x: 4, y: 4, z: 8, core: 2. Of those that a mesh axis runs over, the one named last changes fastest.
Arguments:
- base_field: bfloat16 [64, 128, 128, 128], P(None, 'slab'), may hold values from -6 to 6
- cotangent: bfloat16 [4, 64, 128, 128, 128], P('grp', None, 'slab'), may hold values from -6 to 6
- w_spec: bfloat16 [16, 256, 64, 128], P('grp', 'slab'), may hold values from -0.75 to 0.75
- w_local: bfloat16 [64, 64], replicated, may hold values from -0.75 to 0.75
- bias: float32 [64], replicated, may hold values from -3 to 3
- direction: int32 [64, 30], replicated, may hold values from 0 to 1073741823
- shift: int32 [4, 64], P('grp'), may hold values from 0 to 1073741823
Outputs:
- output: bfloat16 [4, 64, 128, 128, 128], P('grp', None, 'slab')
- d_spec: float32 [16, 256, 64, 128], P('grp', 'slab')
- d_local: float32 [64, 64], replicated
- d_bias: float32 [64], replicated
All inputs are finite; a program needn't handle non-finite values.
Results may differ from a plain program's by a relative error of at most 0.024.
Values may be sent and summed in bfloat16 or wider, within the bound.
A program may use at most 128 MiB of HBM per device.

v0:
```python
from functools import reduce
import math

import jax
import jax.numpy as jnp
from jax import lax
from jax.sharding import PartitionSpec as P

CH = 64
NY = 128
NZ = 128
MODES = 16
BITS = 30


def wave_tables(mode_count, length):
    mode_ids = jnp.arange(mode_count, dtype=jnp.int32)
    kept_ids = jnp.where(mode_ids < mode_count // 2, mode_ids, length - mode_count + mode_ids)
    points = jnp.arange(length, dtype=jnp.int32)
    phases = kept_ids[:, None] * points[None, :] % length
    angles = 2.0 * math.pi / length * phases.astype(jnp.float32)
    return (jnp.cos(angles).astype(jnp.bfloat16), jnp.sin(angles).astype(jnp.bfloat16))


def z_tables(mode_count, length):
    mode_ids = jnp.arange(mode_count, dtype=jnp.int32)
    points = jnp.arange(length, dtype=jnp.int32)
    angles = (
        2.0 * math.pi / length * (mode_ids[:, None] * points[None, :] % length).astype(jnp.float32)
    )
    cos_z, sin_z = (jnp.cos(angles), jnp.sin(angles))
    weight_k = jnp.where(mode_ids == 0, 1.0, 2.0).astype(jnp.float32)[:, None]
    forward = jnp.concatenate([cos_z, -sin_z], 0).T.astype(jnp.bfloat16)
    backward = jnp.concatenate([weight_k * cos_z, -weight_k * sin_z], 0).T.astype(jnp.bfloat16)
    inverse = jnp.stack([weight_k * cos_z, -weight_k * sin_z], 1).astype(jnp.bfloat16)
    return (forward, backward, inverse)


def along_x(pencil, cos_x, sin_x, factor):
    channels = pencil.shape[2] // 2
    flat_rows = pencil.reshape(pencil.shape[0], -1)
    cos_part = jnp.dot(cos_x, flat_rows, preferred_element_type=jnp.float32).reshape(
        -1, pencil.shape[1], pencil.shape[2]
    )
    sin_part = jnp.dot(sin_x, flat_rows, preferred_element_type=jnp.float32).reshape(
        -1, pencil.shape[1], pencil.shape[2]
    )
    real_part = cos_part[..., :channels] + sin_part[..., channels:]
    imag_part = cos_part[..., channels:] - sin_part[..., :channels]
    return (jnp.concatenate([real_part, imag_part], -1) * factor).astype(jnp.bfloat16)


def analyse(values, table_z, cos_y, sin_y, cos_x, sin_x, factor):
    channels, rows_x, span_y, span_z = values.shape
    mode_count = cos_y.shape[0]
    along_z = jnp.dot(values.reshape(-1, span_z), table_z, preferred_element_type=jnp.float32)
    along_z = along_z.astype(jnp.bfloat16).reshape(channels, rows_x, span_y, 2 * mode_count)
    cos_part = jnp.einsum("cxyk,jy->xjkc", along_z, cos_y, preferred_element_type=jnp.float32)
    sin_part = jnp.einsum("cxyk,jy->xjkc", along_z, sin_y, preferred_element_type=jnp.float32)
    real_part = cos_part[:, :, :mode_count] + sin_part[:, :, mode_count:]
    imag_part = cos_part[:, :, mode_count:] - sin_part[:, :, :mode_count]
    joined = jnp.concatenate([real_part, imag_part], -1)
    slab_modes = joined.reshape(rows_x, mode_count * mode_count, 2 * channels).astype(jnp.bfloat16)
    pencil = lax.all_to_all(slab_modes, "slab", split_axis=1, concat_axis=0, tiled=True)
    return along_x(pencil, cos_x, sin_x, factor)


def mix_modes(spectrum, weights, lead):
    channels = weights.shape[2]
    form = lead + "kmc,kmcd->" + lead + "kmd"
    cos_part = jnp.einsum(
        form, spectrum[..., :channels], weights, preferred_element_type=jnp.float32
    )
    sin_part = jnp.einsum(
        form, spectrum[..., channels:], weights, preferred_element_type=jnp.float32
    )
    real_part = cos_part[..., :channels] - sin_part[..., channels:]
    imag_part = cos_part[..., channels:] + sin_part[..., :channels]
    return jnp.concatenate([real_part, imag_part], -1).astype(jnp.bfloat16)


def outer_modes(left_modes, right_modes, lead):
    channels = left_modes.shape[-1] // 2
    form = lead + "kmc," + lead + "kmd->kmcd"
    left_re = left_modes[..., :channels]
    left_im = left_modes[..., channels:]
    right_re = right_modes[..., :channels]
    right_im = right_modes[..., channels:]
    first_half = jnp.einsum(
        form, left_re, right_re, preferred_element_type=jnp.float32
    ) + jnp.einsum(form, left_im, right_im, preferred_element_type=jnp.float32)
    second_half = jnp.einsum(
        form, left_re, right_im, preferred_element_type=jnp.float32
    ) - jnp.einsum(form, left_im, right_re, preferred_element_type=jnp.float32)
    return jnp.concatenate([first_half, second_half], -1)


def synth_x(spectrum, cos_x, sin_x):
    channels = spectrum.shape[2] // 2
    flat_rows = spectrum.reshape(spectrum.shape[0], -1)
    cos_part = jnp.dot(cos_x.T, flat_rows, preferred_element_type=jnp.float32).reshape(
        -1, spectrum.shape[1], spectrum.shape[2]
    )
    sin_part = jnp.dot(sin_x.T, flat_rows, preferred_element_type=jnp.float32).reshape(
        -1, spectrum.shape[1], spectrum.shape[2]
    )
    real_part = cos_part[..., :channels] - sin_part[..., channels:]
    imag_part = cos_part[..., channels:] + sin_part[..., :channels]
    return jnp.concatenate([real_part, imag_part], -1).astype(jnp.bfloat16)


def synth_yz(spectrum, cos_y, sin_y, inverse_z, factor):
    rows_x = spectrum.shape[0]
    channels = spectrum.shape[2] // 2
    mode_count = cos_y.shape[0]
    grid_modes = spectrum.reshape(rows_x, mode_count, mode_count, 2 * channels)
    cos_part = jnp.einsum("xjkd,jy->xykd", grid_modes, cos_y, preferred_element_type=jnp.float32)
    sin_part = jnp.einsum("xjkd,jy->xykd", grid_modes, sin_y, preferred_element_type=jnp.float32)
    real_part = cos_part[..., :channels] - sin_part[..., channels:]
    imag_part = cos_part[..., channels:] + sin_part[..., :channels]
    stacked = jnp.stack([real_part, imag_part], 3).astype(jnp.bfloat16)
    return (
        jnp.einsum("xykrc,krz->cxyz", stacked, inverse_z, preferred_element_type=jnp.float32)
        * factor
    )


def shards(base_field, cotangent, w_spec, w_local, bias, direction, shift):
    full_x = base_field.shape[1] * lax.axis_size("slab")
    group_count = lax.axis_size("grp")
    cos_y, sin_y = wave_tables(MODES, NY)
    cos_x, sin_x = wave_tables(MODES, full_x)
    forward_z, backward_z, inverse_z = z_tables(MODES, NZ)
    fwd_scale = 1.0 / math.sqrt(full_x * NY * NZ)
    inv_scale = 1.0 / math.sqrt(MODES**3)
    grad_scale = 1.0 / math.sqrt(group_count * full_x * NY * NZ)
    number = lax.axis_index("grp") + 1
    gray_code = jnp.bitwise_xor(number, number >> 1)
    picked = [
        jnp.where(gray_code >> bit_pos & 1 == 1, direction[:, bit_pos], 0)
        for bit_pos in range(BITS)
    ]
    mixed_bits = reduce(jnp.bitwise_xor, picked)
    sobol_point = jnp.bitwise_xor(mixed_bits, shift[0]).astype(jnp.float32) * 2.0 ** (-30)
    inputs = (base_field.astype(jnp.float32) * (0.5 + sobol_point)[:, None, None, None]).astype(
        jnp.bfloat16
    )
    modes_u = analyse(inputs, forward_z, cos_y, sin_y, cos_x, sin_x, fwd_scale)
    mixed_modes = mix_modes(modes_u, lax.all_gather(w_spec, "grp", axis=0, tiled=True), "")
    back_x = synth_x(mixed_modes, cos_x, sin_x)
    slab_spec = lax.all_to_all(back_x, "slab", split_axis=0, concat_axis=1, tiled=True)
    spectral = synth_yz(slab_spec, cos_y, sin_y, inverse_z, inv_scale)
    flat_inputs = inputs.reshape(CH, -1)
    local_term = jnp.dot(w_local, flat_inputs, preferred_element_type=jnp.float32).reshape(
        spectral.shape
    )
    pre_act = spectral + local_term + bias[:, None, None, None]
    output = jax.nn.gelu(pre_act).astype(jnp.bfloat16)
    _, pullback = jax.vjp(jax.nn.gelu, pre_act)
    cotan_pre = pullback(cotangent[0].astype(jnp.float32) * grad_scale)[0].astype(jnp.bfloat16)
    flat_cotan = cotan_pre.reshape(CH, -1)
    local_grad = jnp.dot(flat_cotan, flat_inputs.T, preferred_element_type=jnp.float32)
    bias_grad = jnp.sum(flat_cotan.astype(jnp.float32), axis=1)
    d_local, d_bias = lax.psum((local_grad, bias_grad), ("grp", "slab"))
    modes_g = analyse(cotan_pre, backward_z, cos_y, sin_y, cos_x, sin_x, 1.0)
    right_rows = lax.slice_in_dim(modes_g, 0, lax.axis_size("grp") * w_spec.shape[0], axis=0)
    d_spec = lax.psum_scatter(
        outer_modes(modes_u, right_rows, "").astype(jnp.bfloat16),
        "grp",
        scatter_dimension=0,
        tiled=True,
    ).astype(jnp.float32)
    return (output[None], d_spec, d_local, d_bias)


def solution(mesh):
    return jax.shard_map(
        shards,
        mesh=mesh,
        in_specs=(
            P(None, "slab", None, None),
            P("grp", None, "slab", None, None),
            P("grp", "slab", None, None),
            P(),
            P(),
            P(),
            P("grp", None),
        ),
        out_specs=(P("grp", None, "slab", None, None), P("grp", "slab", None, None), P(), P()),
        check_vma=False,
    )
```

profile of v0, /device:TPU:1, one launch (start us, length us, event | category | flops | bytes accessed | tf_op | source)
XLA Modules:
  0.0 210.4 jit_solution(14892243119085806846)
XLA Ops:
  9.2 3.5 %multiply_convert_fusion.1 = bf16[64,2,128,128]{3,2,1,0:T(8,128)(2,1)S(1)} fusion(bf16[64,2,128,128]{3,2,1,0:T(8,128)(2,1)} %param.7, f32[64]{0:T(128)S(1)} %multiply_add_fusion), kind=kLoop, calls=%fused_computation.21 | loop fusion | flops 6291456 | bytes 8388864 | tf_op jit(solution)/shard_map/convert_element_type | solution.py:145
  12.7 1.9 copy-done.2
  14.7 1.5 convolution_convert_fusion.1
  20.0 13.0 %all-to-all-start = ((bf16[2,256,128]{2,0,1:T(2,128)(2,1)}), bf16[2,256,128]{2,0,1:T(2,128)(2,1)S(1)}, u32[]{:S(2)}, u32[]{:S(2)}) async-start(bf16[2,256,128]{2,0,1:T(2,128)(2,1)} %copy.54), calls=%async_computation | async-start | bytes 262144 | tf_op jit(solution)/shard_map/all_to_all | solution.py:64
  33.0 8.8 %fusion.18 = f32[8,8,256,128]{3,1,2,0:T(8,128)} fusion(bf16[64,64]{1,0:T(8,128)(2,1)S(1)} %copy-done, bf16[8,8,256,128]{3,2,1,0:T(8,128)(2,1)} %bitcast.321), kind=kOutput, calls=%fused_computation.29 | convolution fusion | flops 268435456 | bytes 12591104 | tf_op jit(solution)/shard_map/dot_general | solution.py:154
  41.8 2.3 %all-to-all-done = bf16[2,256,128]{2,0,1:T(2,128)(2,1)S(1)} async-done(((bf16[2,256,128]{2,0,1:T(2,128)(2,1)}), bf16[2,256,128]{2,0,1:T(2,128)(2,1)S(1)}, u32[]{:S(2)}, u32[]{:S(2)}) %all-to-all-start) | async-done | bytes 131104 | tf_op jit(solution)/shard_map/all_to_all | solution.py:64
  45.1 1.6 fusion.50
  46.7 1.6 fusion.48
  49.9 8.0 %all-to-all-start.1 = ((bf16[128,4,128]{2,1,0:T(4,128)(2,1)}), bf16[128,4,128]{2,1,0:T(4,128)(2,1)S(1)}, u32[]{:S(2)}, u32[]{:S(2)}) async-start(bf16[128,4,128]{2,1,0:T(4,128)(2,1)} %copy.60), calls=%async_computation.1 | async-start | bytes 262144 | tf_op jit(solution)/shard_map/all_to_all | solution.py:151
  58.0 8.1 %copy.96 = f32[8,8,256,128]{3,2,1,0:T(8,128)} copy(f32[8,8,256,128]{3,1,2,0:T(8,128)} %fusion.18) | data formatting | bytes 16777216
  66.2 2.9 %all-to-all-done.1 = bf16[128,4,128]{2,1,0:T(4,128)(2,1)S(1)} async-done(((bf16[128,4,128]{2,1,0:T(4,128)(2,1)}), bf16[128,4,128]{2,1,0:T(4,128)(2,1)S(1)}, u32[]{:S(2)}, u32[]{:S(2)}) %all-to-all-start.1) | async-done | bytes 131104 | tf_op jit(solution)/shard_map/all_to_all | solution.py:151
  70.9 2.2 %copy-done.4 = f32[8,8,256,128]{3,2,1,0:T(8,128)S(1)} copy-done((f32[8,8,256,128]{3,2,1,0:T(8,128)S(1)}, f32[8,8,256,128]{3,2,1,0:T(8,128)}, u32[]{:S(2)}) %copy-start.4) | copy-done | bytes 8388632
  73.1 13.5 %convert_reduce_fusion = (f32[64]{0:T(128)S(1)}, bf16[64,2,128,128]{3,2,0,1:T(8,128)(2,1)S(1)}, bf16[1,64,2,128,128]{4,3,1,2,0:T(8,128)(2,1)}) fusion(bf16[1,64,2,128,128]{4,3,2,1,0:T(8,128)(2,1)} %param.8, f32[64]{0:T(128)S(1)} %copy-done.7, f32[64,2,128,128]{3,2,1,0:T(8,128)S(1)} %bitcast.323, bf16[2,128,16,2,64]{1,4,2,0,3:T(8,128)(2,1)S(1)} %pad_maximum_fusion, ...), kind=kOutput, calls=%fused_computation.19 | convolution fusion | flops 195051456 | bytes 22028800 | tf_op jit(solution)/shard_map/xykrc,krz->cxyz/dot_general | solution.py:123
  87.2 1.4 copy-done.5
  88.6 1.5 convolution_convert_fusion
  93.9 7.4 %all-to-all-start.2 = ((bf16[2,256,128]{2,0,1:T(2,128)(2,1)}), bf16[2,256,128]{2,0,1:T(2,128)(2,1)S(1)}, u32[]{:S(2)}, u32[]{:S(2)}) async-start(bf16[2,256,128]{2,0,1:T(2,128)(2,1)} %copy.73), calls=%async_computation.2 | async-start | bytes 262144 | tf_op jit(solution)/shard_map/all_to_all | solution.py:64
  101.7 10.8 %all-to-all-done.2 = bf16[2,256,128]{2,0,1:T(2,128)(2,1)S(1)} async-done(((bf16[2,256,128]{2,0,1:T(2,128)(2,1)}), bf16[2,256,128]{2,0,1:T(2,128)(2,1)S(1)}, u32[]{:S(2)}, u32[]{:S(2)}) %all-to-all-start.2) | async-done | bytes 131104 | tf_op jit(solution)/shard_map/all_to_all | solution.py:64
  113.4 1.3 add_convert_fusion
  114.6 1.7 pad_maximum_fusion.1
  116.4 5.1 %copy.82 = bf16[1,64,2,128,128]{4,3,2,1,0:T(8,128)(2,1)} copy(bf16[1,64,2,128,128]{4,3,1,2,0:T(8,128)(2,1)} %get-tuple-element.20) | data formatting | bytes 8388608
  121.4 1.1 copy-done.6
  122.6 4.7 %fusion.21 = f32[64,64]{1,0:T(8,128)S(1)} fusion(bf16[64,2,128,128]{3,2,1,0:T(8,128)(2,1)S(1)} %copy-done.3, bf16[64,2,128,128]{3,2,0,1:T(8,128)(2,1)S(1)} %copy-done.6), kind=kOutput, calls=%fused_computation.38 | convolution fusion | flops 268435456 | bytes 8404992 | tf_op jit(solution)/shard_map/dot_general | solution.py:162
  127.3 74.5 %all-reduce = (f32[64,64]{1,0:T(8,128)}, f32[64]{0:T(128)}) all-reduce(f32[64,64]{1,0:T(8,128)S(1)} %fusion.21, f32[64]{0:T(128)S(1)} %get-tuple-element.18), channel_id=1, replica_groups=mesh['grp'=4,'slab'=64] {'grp','slab'}, use_global_device_ids=true, to_apply=%region_1.2 | all-reduce | flops 4160 | bytes 33280 | tf_op jit(solution)/shard_map/psum | solution.py:164
  201.7 1.8 convert_element_type.156
  (73 shorter events, 15.7 us)
Async XLA Ops:
  7.2 25.8 %copy-start = (bf16[64,64]{1,0:T(8,128)(2,1)S(1)}, bf16[64,64]{1,0:T(8,128)(2,1)}, u32[]{:S(2)}) copy-start(bf16[64,64]{1,0:T(8,128)(2,1)} %param.10) | copy-start | bytes 24580
  7.2 37.9 %all-gather.2.cloned.1.call-start = ((), (), s32[]{:S(2)}) async-start(), calls=%async_computation.4 | async-start | bytes 1310720 | tf_op jit(solution)/shard_map/all_gather | solution.py:149
  12.7 1.9 copy-start.2
  20.0 24.1 %all-to-all-start = ((bf16[2,256,128]{2,0,1:T(2,128)(2,1)}), bf16[2,256,128]{2,0,1:T(2,128)(2,1)S(1)}, u32[]{:S(2)}, u32[]{:S(2)}) async-start(bf16[2,256,128]{2,0,1:T(2,128)(2,1)} %copy.54), calls=%async_computation | async-start | bytes 262144 | tf_op jit(solution)/shard_map/all_to_all | solution.py:64
  49.9 19.1 %all-to-all-start.1 = ((bf16[128,4,128]{2,1,0:T(4,128)(2,1)}), bf16[128,4,128]{2,1,0:T(4,128)(2,1)S(1)}, u32[]{:S(2)}, u32[]{:S(2)}) async-start(bf16[128,4,128]{2,1,0:T(4,128)(2,1)} %copy.60), calls=%async_computation.1 | async-start | bytes 262144 | tf_op jit(solution)/shard_map/all_to_all | solution.py:151
  69.7 3.4 %copy-start.4 = (f32[8,8,256,128]{3,2,1,0:T(8,128)S(1)}, f32[8,8,256,128]{3,2,1,0:T(8,128)}, u32[]{:S(2)}) copy-start(f32[8,8,256,128]{3,2,1,0:T(8,128)} %copy.96) | copy-start | bytes 25165828
  70.3 2.8 %copy-start.7 = (f32[64]{0:T(128)S(1)}, f32[64]{0:T(128)}, u32[]{:S(2)}) copy-start(f32[64]{0:T(128)} %param.11) | copy-start | bytes 772
  86.7 1.9 copy-start.5
  93.9 18.6 %all-to-all-start.2 = ((bf16[2,256,128]{2,0,1:T(2,128)(2,1)}), bf16[2,256,128]{2,0,1:T(2,128)(2,1)S(1)}, u32[]{:S(2)}, u32[]{:S(2)}) async-start(bf16[2,256,128]{2,0,1:T(2,128)(2,1)} %copy.73), calls=%async_computation.2 | async-start | bytes 262144 | tf_op jit(solution)/shard_map/all_to_all | solution.py:64
  101.4 100.3 %reduce-scatter.2.cloned.1.call-start = ((), (), s32[]{:S(2)}) async-start(), calls=%async_computation.5 | async-start | bytes 1310720 | tf_op jit(solution)/shard_map/reduce_scatter | solution.py:167
  116.3 5.1 %copy-start.3 = (bf16[64,2,128,128]{3,2,1,0:T(8,128)(2,1)S(1)}, bf16[64,2,128,128]{3,2,1,0:T(8,128)(2,1)}, u32[]{:S(2)}) copy-start(bf16[64,2,128,128]{3,2,1,0:T(8,128)(2,1)} %copy-done.2) | copy-start | bytes 12582916
  116.4 6.2 %copy-start.6 = (bf16[64,2,128,128]{3,2,0,1:T(8,128)(2,1)S(1)}, bf16[64,2,128,128]{3,2,0,1:T(8,128)(2,1)}, u32[]{:S(2)}) copy-start(bf16[64,2,128,128]{3,2,0,1:T(8,128)(2,1)} %copy-done.5) | copy-start | bytes 12582916
  116.4 87.2 %copy-start.1 = (bf16[64,64]{1,0:T(8,128)(2,1)S(1)}, bf16[64,64]{1,0:T(8,128)(2,1)}, u32[]{:S(2)}) copy-start(bf16[64,64]{1,0:T(8,128)(2,1)} %param.10) | copy-start | bytes 24580
Sparse Core Ops, SparseCore 0:
  9.8 29.4 all-gather.1
  116.5 19.5 reduce-scatter.1
where the time goes:
time: 211 us; the launch traced here: 210 us
  blocking collectives  74.5 us (35%)
  matrix products  39.9 us (19%)
  starting transfers between devices  28.7 us (14%)
  local copies, waits for them, and re-layouts  25 us (12%)
  waiting for transfers between devices  16.7 us (8%)
  between operations  14.5 us (7%)
  other arithmetic  11.2 us (5%)
    psum x1, blocking collectives, shards(): d_local, d_bias = lax.psum((local_grad, bias_grad), ('grp', 'slab'))  74.5 us
    all_to_all x2, starting transfers between devices, analyse(): lax.all_to_all(slab_modes, 'slab', split_axis=1, concat_axis=0, tiled=True)  20.4 us
    unnamed x20, local copies, waits for them, and re-layouts  19.9 us
    dot_general x1, matrix products, synth_yz(): jnp.einsum('xykrc,krz->cxyz', stacked, inverse_z, preferred_element_type=...  13.5 us
    all_to_all x2, waiting for transfers between devices, analyse(): lax.all_to_all(slab_modes, 'slab', split_axis=1, concat_axis=0, tiled=True)  13.1 us
    dot_general x1, matrix products, shards(): jnp.dot(w_local, flat_inputs, preferred_element_type=jnp.float32)  8.8 us
    all_to_all x1, starting transfers between devices, shards(): lax.all_to_all(back_x, 'slab', split_axis=0, concat_axis=1, tiled=True)  8.01 us
    dot_general x1, matrix products, shards(): jnp.dot(flat_cotan, flat_inputs.T, preferred_element_type=jnp.float32)  4.67 us
  transfers between devices with their start and end apart: 5, of which 3 were waited for; matrix products, arithmetic and copies ran while one was open for 18% of the time, Pallas kernels for 0%

commit v1 on v0

v1 whole, which is shorter than its diff:
```python
from functools import reduce
import math

import jax
import jax.numpy as jnp
import ml_dtypes
import numpy as np
from jax import lax
from jax.experimental import pallas as pl
from jax.experimental.pallas import tpu as pltpu
from jax.sharding import PartitionSpec as P

CH = 64
NX = 128
NY = 128
NZ = 128
MODES = 16
BITS = 30
N_GRP = 4
N_SLAB = 64
N_LOW = 8
N_Z = 8
MESH = pl.DeviceIdType.MESH
F32 = jnp.float32
BF16 = jnp.bfloat16
MIB = 1024 * 1024


def waves(length, half):
    ids = np.arange(MODES)
    if not half:
        ids = np.where(ids < MODES // 2, ids, length - MODES + ids)
    angles = 2.0 * math.pi / length * (ids[:, None] * np.arange(length)[None, :] % length)
    return np.cos(angles), np.sin(angles)


def as_bf16(table):
    return np.asarray(table, np.float32).astype(ml_dtypes.bfloat16)


def table_ty():
    cos_y, sin_y = waves(NY, False)
    out = np.zeros((2, 2, MODES, 2, NY))
    for c2 in range(2):
        out[0, c2, :, c2] = cos_y
        out[1, c2, :, c2] = sin_y
    return as_bf16(out.reshape(64, 256))


def weights_z(backward):
    return np.where(np.arange(MODES) == 0, 1.0, 2.0 if backward else 1.0)[:, None]


def table_zt(backward):
    cos_z, sin_z = waves(NZ, True)
    weight = weights_z(backward)
    cos_z = (weight * cos_z).reshape(4, 4, NZ)
    sin_z = (weight * sin_z).reshape(4, 4, NZ)
    out = np.zeros((2, 4, 2, 4, 2, 2, NZ))
    for x in range(2):
        out[0, :, x, :, 0, x] = cos_z
        out[0, :, x, :, 1, x] = -sin_z
        out[1, :, x, :, 0, x] = -sin_z
        out[1, :, x, :, 1, x] = -cos_z
    return as_bf16(out.reshape(64, 512))


def table_tx():
    cos_x, sin_x = waves(NX, False)
    out = np.zeros((2, MODES, 4, NX, 4))
    for m in range(4):
        out[0, :, m, :, m] = cos_x
        out[1, :, m, :, m] = sin_x
    return as_bf16(out.reshape(128, 512))


def table_ey():
    cos_y, sin_y = waves(NY, False)
    out = np.zeros((2, NY, 2, 2, MODES))
    for c2 in range(2):
        out[c2, :, c2, 0] = cos_y.T
        out[c2, :, c2, 1] = -sin_y.T
    return as_bf16(out.reshape(256, 64))


def table_ez():
    cos_z, sin_z = waves(NZ, True)
    weight = weights_z(True) / math.sqrt(MODES**3)
    cos_z = (weight * cos_z).reshape(4, 4, NZ)
    sin_z = (weight * sin_z).reshape(4, 4, NZ)
    out = np.zeros((2, 4, 2, 4, 2, 2, NZ))
    for x in range(2):
        out[0, :, x, :, 0, x] = cos_z
        out[1, :, x, :, 0, x] = -sin_z
        out[0, :, x, :, 1, x] = sin_z
        out[1, :, x, :, 1, x] = cos_z
    return as_bf16(out.reshape(64, 512))


def lane_sign(rows, first, second):
    lane = lax.broadcasted_iota(jnp.int32, (rows, 128), 1)
    return jnp.where(lane < 64, first, second).astype(F32)


def turned(rows, first, second):
    return pltpu.roll(rows, 64, 1) * lane_sign(rows.shape[0], first, second)


def nt_dot(left, right, precision=None):
    return lax.dot_general(
        left, right, (((1,), (1,)), ((), ())), preferred_element_type=F32, precision=precision
    )


def fetch_field(field, held, sems):
    for part in range(8):
        rows = pl.ds(8 * part, 8)
        pltpu.make_async_copy(field.at[rows], held.at[rows], sems.at[part]).start()


def analyse(field, held, sems, ty_ref, zt_ref, along_y, slab_modes):

    def channels(part, carry):
        rows = pl.ds(8 * part, 8)
        pltpu.make_async_copy(field.at[rows], held.at[rows], sems.at[part]).wait()
        for pair in range(4):
            first = 8 * part + 2 * pair
            cells = jnp.concatenate(
                [
                    jnp.concatenate([held[first + c2, 0], held[first + c2, 1]], 1)
                    for c2 in range(2)
                ],
                0,
            )
            got = jnp.dot(ty_ref[...], cells, preferred_element_type=F32)
            for cs in range(2):
                for c2 in range(2):
                    at = cs * 32 + c2 * 16
                    for x in range(2):
                        start = (2 * cs + x) * 1024 + first + c2
                        along_y[pl.ds(start, 16, stride=64), :] = got[
                            at : at + 16, x * 128 : x * 128 + 128
                        ]
        return carry

    lax.fori_loop(0, 8, channels, 0)
    for quarter in range(4):
        rows = jnp.concatenate(
            [
                along_y[part * 1024 + quarter * 256 : part * 1024 + quarter * 256 + 256, :]
                for part in range(4)
            ],
            1,
        ).astype(BF16)
        got = nt_dot(zt_ref[...], rows)
        for jy in range(4):
            real = got[0:32, jy * 64 : jy * 64 + 64]
            imag = got[32:64, jy * 64 : jy * 64 + 64]
            owner = (quarter * 4 + jy) * 4
            slab_modes[owner : owner + 4] = (
                jnp.concatenate([real, imag], 1).reshape(4, 8, 128).astype(BF16)
            )


def greet(barrier, me, grp):
    def tell(step, carry):
        pl.semaphore_signal(
            barrier, inc=1, device_id={"slab": lax.rem(me + step, N_SLAB)}, device_id_type=MESH
        )
        return carry

    lax.fori_loop(1, N_SLAB, tell, 0)
    for step in range(1, N_GRP):
        pl.semaphore_signal(
            barrier, inc=1, device_id={"grp": lax.rem(grp + step, N_GRP)}, device_id_type=MESH
        )


def send_all(source, target, send_sem, recv_sem, me):
    low = lax.rem(me, N_LOW)
    z = me // N_LOW
    for dz in (4, 3, 5, 2, 6, 1, 7, 0):

        def go(step, carry):
            other = lax.rem(z + dz, N_Z) * N_LOW + lax.rem(low + step, N_LOW)
            pltpu.make_async_remote_copy(
                src_ref=source.at[other],
                dst_ref=target.at[me],
                send_sem=send_sem,
                recv_sem=recv_sem,
                device_id={"slab": other},
                device_id_type=MESH,
            ).start()
            return carry

        lax.fori_loop(1 if dz == 0 else 0, N_LOW, go, 0)
    target[pl.ds(me, 1)] = source[pl.ds(me, 1)]


def wait_blocks(source, target, send_sem, recv_sem, count, me):
    pltpu.make_async_remote_copy(
        src_ref=source.at[pl.ds(0, count)],
        dst_ref=target.at[pl.ds(0, count)],
        send_sem=send_sem,
        recv_sem=recv_sem,
        device_id={"slab": me},
        device_id_type=MESH,
    ).wait()


def send_grp(source, target, send_sem, recv_sem, grp, by_target):
    for step in range(1, N_GRP):
        other = lax.rem(grp + step, N_GRP)
        pltpu.make_async_remote_copy(
            src_ref=source.at[other] if by_target else source.at[grp],
            dst_ref=target.at[grp],
            send_sem=send_sem,
            recv_sem=recv_sem,
            device_id={"grp": other},
            device_id_type=MESH,
        ).start()


def x_modes(pencil, tx_ref):
    rows = pencil[...].astype(F32).reshape(512, 128).astype(BF16)
    both = jnp.dot(tx_ref[...], rows, preferred_element_type=F32)
    return both[:64] + turned(both[64:], 1.0, -1.0)


def spectral_kernel(
    field, w_ref, wl_ref, scale_ref, ty_ref, zt_ref, tx_ref, txb_ref,
    grid_modes, own_modes, scales, kron_ref,
    held, along_y, slab_modes, pencil, mixed, gathered, back, landed, all_modes, scale_own, scale_all, w_two,
    field_sems, send_sems, recv_sems,
):
    me = lax.axis_index("slab")
    grp = lax.axis_index("grp")
    barrier = pltpu.get_barrier_semaphore()
    fetch_field(field, held, field_sems)
    greet(barrier, me, grp)
    analyse(field, held, field_sems, ty_ref, zt_ref, along_y, slab_modes)
    scale_own[grp] = scale_ref[...]
    scale_all[grp] = scale_ref[...]
    pl.semaphore_wait(barrier, N_SLAB - 1 + N_GRP - 1)
    send_all(slab_modes, pencil, send_sems.at[0], recv_sems.at[0], me)
    send_grp(scale_own, scale_all, send_sems.at[1], recv_sems.at[1], grp, False)
    for k in range(16):
        block = w_ref[k].astype(F32)
        w_two[k * 128 : k * 128 + 64, :] = w_ref[k]
        w_two[k * 128 + 64 : k * 128 + 128, :] = turned(block, -1.0, 1.0).astype(BF16)
    local = (wl_ref[...].astype(F32) * scale_ref[0:1, 0:64]).astype(BF16)
    pick = (
        lax.broadcasted_iota(jnp.int32, (64, 512), 0)
        == lax.broadcasted_iota(jnp.int32, (64, 512), 1) // 8
    )
    wide = jnp.dot(local, pick.astype(F32).astype(BF16), preferred_element_type=F32).astype(BF16)
    row_pick = (
        lax.broadcasted_iota(jnp.int32, (64, 64), 0) // 8
        == lax.broadcasted_iota(jnp.int32, (64, 64), 1)
    )
    same = (
        lax.broadcasted_iota(jnp.int32, (64, 512), 0) % 8
        == lax.broadcasted_iota(jnp.int32, (64, 512), 1) % 8
    )
    row_ids = lax.broadcasted_iota(jnp.int32, (64, 64), 0) // 8
    col_ids = lax.broadcasted_iota(jnp.int32, (64, 64), 1)
    for octet in range(8):
        rows_of = (row_ids + 8 * octet == col_ids).astype(F32).astype(BF16)
        tall = jnp.dot(rows_of, wide, preferred_element_type=F32)
        kron_ref[octet * 64 : octet * 64 + 64, :] = jnp.where(same, tall, 0.0).astype(BF16)
    pltpu.make_async_remote_copy(
        src_ref=scale_own.at[pl.ds(0, N_GRP - 1)],
        dst_ref=scale_all.at[pl.ds(0, N_GRP - 1)],
        send_sem=send_sems.at[1],
        recv_sem=recv_sems.at[1],
        device_id={"slab": me},
        device_id_type=MESH,
    ).wait()
    scales[...] = scale_all[...]
    wait_blocks(slab_modes, pencil, send_sems.at[0], recv_sems.at[0], N_SLAB - 1, me)
    all_modes[...] = x_modes(pencil, tx_ref) * (1.0 / math.sqrt(NX * NY * NZ))
    own = all_modes[pl.ds(pl.multiple_of(16 * grp, 16), 16), :]
    own_modes[...] = own
    shifted = jnp.concatenate([own * scale_all[s, 0:1, :] for s in range(N_GRP)], 0)
    row_mode = lax.broadcasted_iota(jnp.int32, (64, 128), 0) % 16
    spread = jnp.concatenate(
        [jnp.where(row_mode == k, shifted, 0.0).astype(BF16) for k in range(16)], 1
    )
    mixed[...] = (
        jnp.dot(spread, w_two[...], preferred_element_type=F32).astype(BF16).reshape(4, 16, 128)
    )
    send_grp(mixed, gathered, send_sems.at[2], recv_sems.at[2], grp, True)
    gathered[pl.ds(grp, 1)] = mixed[pl.ds(grp, 1)]
    wait_blocks(mixed, gathered, send_sems.at[2], recv_sems.at[2], N_GRP - 1, me)
    full = gathered[...].reshape(64, 128)
    both = jnp.concatenate([full, turned(full.astype(F32), -1.0, 1.0).astype(BF16)], 0)
    cells = jnp.dot(txb_ref[...], both, preferred_element_type=F32)
    back[...] = cells.reshape(64, 8, 128).astype(BF16)
    send_all(back, landed, send_sems.at[3], recv_sems.at[3], me)
    wait_blocks(back, landed, send_sems.at[3], recv_sems.at[3], N_SLAB - 1, me)
    grid_modes[...] = landed[...]


def spectral_call(field, w_spec, w_local, scale_rows):
    vmem = pl.BlockSpec(memory_space=pltpu.VMEM)
    return pl.pallas_call(
        spectral_kernel,
        out_shape=(
            jax.ShapeDtypeStruct((64, 8, 128), BF16),
            jax.ShapeDtypeStruct((16, 128), F32),
            jax.ShapeDtypeStruct((4, 8, 128), F32),
            jax.ShapeDtypeStruct((512, 512), BF16),
        ),
        in_specs=[pl.BlockSpec(memory_space=pl.ANY)] + [vmem] * 7,
        out_specs=(vmem,) * 4,
        scratch_shapes=[
            pltpu.VMEM((64, 2, 128, 128), BF16),
            pltpu.VMEM((4096, 128), F32),
            pltpu.VMEM((64, 8, 128), BF16),
            pltpu.VMEM((64, 8, 128), BF16),
            pltpu.VMEM((4, 16, 128), BF16),
            pltpu.VMEM((4, 16, 128), BF16),
            pltpu.VMEM((64, 8, 128), BF16),
            pltpu.VMEM((64, 8, 128), BF16),
            pltpu.VMEM((64, 128), F32),
            pltpu.VMEM((4, 8, 128), F32),
            pltpu.VMEM((4, 8, 128), F32),
            pltpu.VMEM((2048, 128), BF16),
            pltpu.SemaphoreType.DMA((8,)),
            pltpu.SemaphoreType.DMA((4,)),
            pltpu.SemaphoreType.DMA((4,)),
        ],
        compiler_params=pltpu.CompilerParams(
            collective_id=0, has_side_effects=True, vmem_limit_bytes=32 * MIB
        ),
    )(
        field, w_spec, w_local, scale_rows,
        table_ty(), table_zt(False), table_tx(), np.ascontiguousarray(table_tx().T),
    )


GELU_K = math.sqrt(2.0 / math.pi)
GELU_A = GELU_K * 0.044715


def cells_kernel(
    grid_modes, kron_ref, bias_ref, scale_ref, ey_ref, ez_ref, field_ref, cotan_ref,
    out_ref, cotan_pre_ref, sums_ref,
    along_z, spectral, local, field_rows, cotan_rows, grad, bias_sum,
):
    step = pl.program_id(0)
    grad_scale = 1.0 / math.sqrt(N_GRP * NX * NY * NZ)

    @pl.when(step == 0)
    def _():
        grad[...] = jnp.zeros_like(grad)
        bias_sum[...] = jnp.zeros_like(bias_sum)
        for quarter in range(4):
            rows = grid_modes[quarter * 16 : quarter * 16 + 16].astype(F32).reshape(128, 128)
            turn = rows.T
            per_c = jnp.concatenate(
                [
                    jnp.concatenate(
                        [turn[0:64, jy * 32 : jy * 32 + 32], turn[64:128, jy * 32 : jy * 32 + 32]],
                        1,
                    )
                    for jy in range(4)
                ],
                0,
            ).astype(BF16)
            got = jnp.dot(per_c, ez_ref[...], preferred_element_type=F32)
            for jy in range(4):
                for cs in range(2):
                    for x in range(2):
                        start = x * 2048 + cs * 16 + quarter * 4 + jy
                        lane = cs * 256 + x * 128
                        along_z[pl.ds(start, 64, stride=32), :] = got[
                            jy * 64 : jy * 64 + 64, lane : lane + 128
                        ]

        def pair(index, carry):
            rows = jnp.concatenate(
                [
                    along_z[pl.ds(pl.multiple_of(x * 2048 + 64 * index, 64), 64), :]
                    for x in range(2)
                ],
                1,
            ).astype(BF16)
            got = jnp.dot(ey_ref[...], rows, preferred_element_type=F32)
            spectral[2 * index] = got[:128] + bias_ref[2 * index]
            spectral[2 * index + 1] = got[128:] + bias_ref[2 * index + 1]
            return carry

        lax.fori_loop(0, 32, pair, 0)

    halves = []
    for x in range(2):
        halves.append(field_ref[:, x].astype(F32))
    for half in range(2):
        rows = jnp.concatenate(
            [part[:, 8 * half : 8 * half + 8].reshape(512, 128) for part in halves], 1
        ).astype(BF16)
        field_rows[:, half * 256 : half * 256 + 256] = rows
        got = jnp.dot(kron_ref[...], rows, preferred_element_type=F32)
        local[:, 8 * half : 8 * half + 8, :] = got.reshape(64, 8, 256)

    def few(index, carry):
        at = pl.ds(4 * index, 4)
        y_at = pl.ds(pl.multiple_of(16 * step, 16), 16)
        sums = jnp.zeros((4, 8, 128), F32)
        for x in range(2):
            lanes = slice(x * 128, x * 128 + 128)
            pre = local[at, :, lanes] + spectral[at, y_at, lanes]
            square = pre * pre
            half_tanh = 0.5 + 0.5 * jnp.tanh(pre * (GELU_K + GELU_A * square))
            out_ref[at, x] = (pre * half_tanh).astype(BF16)
            slope = half_tanh * (
                1.0
                + (1.0 - half_tanh) * (pre * (2.0 * GELU_K + 6.0 * GELU_A * square))
            )
            cotan = (slope * (cotan_ref[at, x].astype(F32) * grad_scale)).astype(BF16)
            cotan_pre_ref[at, x] = cotan
            wide = cotan.astype(F32)
            for half in range(2):
                rows = wide[:, 8 * half : 8 * half + 8]
                sums = sums + rows
                cotan_rows[
                    pl.ds(pl.multiple_of(32 * index, 32), 32),
                    half * 256 + x * 128 : half * 256 + x * 128 + 128,
                ] = rows.reshape(32, 128).astype(BF16)
        bias_sum[at] += sums
        return carry

    lax.fori_loop(0, 16, few, 0)
    grad[...] += nt_dot(cotan_rows[...], field_rows[...])

    @pl.when(step == pl.num_programs(0) - 1)
    def _():
        same = (
            lax.broadcasted_iota(jnp.int32, (512, 512), 0) % 8
            == lax.broadcasted_iota(jnp.int32, (512, 512), 1) % 8
        )
        per_c = jnp.sum(jnp.where(same, grad[...], 0.0).reshape(64, 8, 512), axis=1)
        pick = (
            lax.broadcasted_iota(jnp.int32, (512, 64), 0) // 8
            == lax.broadcasted_iota(jnp.int32, (512, 64), 1)
        ).astype(F32)
        d_local = jnp.dot(
            per_c, pick, preferred_element_type=F32, precision=lax.Precision.HIGHEST
        )
        d_local = d_local * scale_ref[0:1, 0:64]
        lanes = jnp.sum(bias_sum[...], axis=1)
        d_bias = nt_dot(jnp.ones((8, 128), F32), lanes, lax.Precision.HIGHEST)
        side = jnp.concatenate([d_bias, jnp.zeros((56, 64), F32)], 0)
        sums_ref[...] = jnp.concatenate([d_local, side], 1).reshape(8, 8, 128)


def cells_call(grid_modes, kron, bias, scale_rows, field, cotangent):
    vmem = pl.BlockSpec(memory_space=pltpu.VMEM)
    block = pl.BlockSpec((64, 2, 16, 128), lambda step: (0, 0, step, 0))
    cells = 64 * 2 * 128 * 128
    return pl.pallas_call(
        cells_kernel,
        grid=(8,),
        out_shape=(
            jax.ShapeDtypeStruct((64, 2, 128, 128), BF16),
            jax.ShapeDtypeStruct((64, 2, 128, 128), BF16),
            jax.ShapeDtypeStruct((8, 8, 128), F32),
        ),
        in_specs=[
            vmem, vmem, pl.BlockSpec(memory_space=pltpu.SMEM), vmem, vmem, vmem, block, block,
        ],
        out_specs=(block, block, pl.BlockSpec((8, 8, 128), lambda step: (0, 0, 0))),
        scratch_shapes=[
            pltpu.VMEM((4096, 128), F32),
            pltpu.VMEM((64, 128, 256), F32),
            pltpu.VMEM((64, 16, 256), F32),
            pltpu.VMEM((512, 512), BF16),
            pltpu.VMEM((512, 512), BF16),
            pltpu.VMEM((512, 512), F32),
            pltpu.VMEM((64, 8, 128), F32),
        ],
        compiler_params=pltpu.CompilerParams(vmem_limit_bytes=40 * MIB),
        cost_estimate=pl.CostEstimate(
            flops=cells * 64 * 8 * 4, bytes_accessed=cells * 8, transcendentals=cells
        ),
    )(grid_modes, kron, bias, scale_rows, table_ey(), table_ez(), field, cotangent)


def gradient_kernel(
    cotan, sums_ref, ty_ref, zt_ref, tx_ref,
    modes_out, sums_out,
    held, along_y, slab_modes, pencil, modes, gathered, own_sums, first, second, second_own, third,
    field_sems, send_sems, recv_sems,
):
    me = lax.axis_index("slab")
    grp = lax.axis_index("grp")
    low = lax.rem(me, N_LOW)
    z = me // N_LOW
    barrier = pltpu.get_barrier_semaphore()
    fetch_field(cotan, held, field_sems)
    greet(barrier, me, grp)
    for g_step in range(1, N_GRP):

        def tell(step, carry):
            pl.semaphore_signal(
                barrier,
                inc=1,
                device_id={
                    "grp": lax.rem(grp + g_step, N_GRP),
                    "slab": z * N_LOW + lax.rem(low + step, N_LOW),
                },
                device_id_type=MESH,
            )
            return carry

        lax.fori_loop(1, N_LOW, tell, 0)
    analyse(cotan, held, field_sems, ty_ref, zt_ref, along_y, slab_modes)
    own_sums[...] = sums_ref[...]
    pl.semaphore_wait(barrier, N_SLAB - 1 + N_GRP - 1 + (N_GRP - 1) * (N_LOW - 1))

    def scatter(step, carry):
        other = lax.rem(z + step, N_Z)
        pltpu.make_async_remote_copy(
            src_ref=own_sums.at[other],
            dst_ref=first.at[z],
            send_sem=send_sems.at[1],
            recv_sem=recv_sems.at[1],
            device_id={"slab": other * N_LOW + low},
            device_id_type=MESH,
        ).start()
        return carry

    lax.fori_loop(1, N_Z, scatter, 0)
    first[pl.ds(z, 1)] = own_sums[pl.ds(z, 1)]
    send_all(slab_modes, pencil, send_sems.at[0], recv_sems.at[0], me)
    wait_blocks(own_sums, first, send_sems.at[1], recv_sems.at[1], N_Z - 1, me)
    part = jnp.sum(first[...], axis=0, keepdims=True)
    mine = grp * N_LOW + low
    second[pl.ds(mine, 1)] = part
    second_own[...] = part
    for g_step in range(N_GRP):

        def spread(step, carry):
            pltpu.make_async_remote_copy(
                src_ref=second_own.at[0],
                dst_ref=second.at[mine],
                send_sem=send_sems.at[2],
                recv_sem=recv_sems.at[2],
                device_id={
                    "grp": lax.rem(grp + g_step, N_GRP),
                    "slab": z * N_LOW + lax.rem(low + step, N_LOW),
                },
                device_id_type=MESH,
            ).start()
            return carry

        lax.fori_loop(1 if g_step == 0 else 0, N_LOW, spread, 0)
    wait_blocks(slab_modes, pencil, send_sems.at[0], recv_sems.at[0], N_SLAB - 1, me)
    modes[...] = x_modes(pencil, tx_ref).astype(BF16).reshape(4, 16, 128)
    send_grp(modes, gathered, send_sems.at[3], recv_sems.at[3], grp, True)
    gathered[pl.ds(grp, 1)] = modes[pl.ds(grp, 1)]
    wait_blocks(second, second, send_sems.at[2], recv_sems.at[2], N_GRP * N_LOW - 1, me)
    third[pl.ds(z, 1)] = jnp.sum(second[...], axis=0, keepdims=True)

    def collect(step, carry):
        other = lax.rem(z + step, N_Z)
        pltpu.make_async_remote_copy(
            src_ref=third.at[z],
            dst_ref=third.at[z],
            send_sem=send_sems.at[4],
            recv_sem=recv_sems.at[4],
            device_id={"slab": other * N_LOW + low},
            device_id_type=MESH,
        ).start()
        return carry

    lax.fori_loop(1, N_Z, collect, 0)
    wait_blocks(modes, gathered, send_sems.at[3], recv_sems.at[3], N_GRP - 1, me)
    modes_out[...] = gathered[...]
    wait_blocks(third, third, send_sems.at[4], recv_sems.at[4], N_Z - 1, me)
    sums_out[...] = third[...]


def gradient_call(cotan, sums):
    vmem = pl.BlockSpec(memory_space=pltpu.VMEM)
    return pl.pallas_call(
        gradient_kernel,
        out_shape=(
            jax.ShapeDtypeStruct((4, 16, 128), BF16),
            jax.ShapeDtypeStruct((8, 8, 128), F32),
        ),
        in_specs=[pl.BlockSpec(memory_space=pl.ANY)] + [vmem] * 4,
        out_specs=(vmem,) * 2,
        scratch_shapes=[
            pltpu.VMEM((64, 2, 128, 128), BF16),
            pltpu.VMEM((4096, 128), F32),
            pltpu.VMEM((64, 8, 128), BF16),
            pltpu.VMEM((64, 8, 128), BF16),
            pltpu.VMEM((4, 16, 128), BF16),
            pltpu.VMEM((4, 16, 128), BF16),
            pltpu.VMEM((8, 8, 128), F32),
            pltpu.VMEM((8, 8, 128), F32),
            pltpu.VMEM((32, 8, 128), F32),
            pltpu.VMEM((1, 8, 128), F32),
            pltpu.VMEM((8, 8, 128), F32),
            pltpu.SemaphoreType.DMA((8,)),
            pltpu.SemaphoreType.DMA((5,)),
            pltpu.SemaphoreType.DMA((5,)),
        ],
        compiler_params=pltpu.CompilerParams(
            collective_id=1, has_side_effects=True, vmem_limit_bytes=32 * MIB
        ),
    )(cotan, sums, table_ty(), table_zt(True), table_tx())


def weights_kernel(modes_g, own_modes, scales, sums_ref, d_spec, d_local, d_bias):
    own = own_modes[...]
    shifted = jnp.concatenate([own * scales[s, 0:1, :] for s in range(N_GRP)], 0)
    columns = shifted.T
    rows = modes_g[...].astype(F32).reshape(64, 128)
    other = turned(rows, 1.0, -1.0)
    for k in range(16):
        total = jnp.zeros((64, 128), F32)
        for s in range(N_GRP):
            at = s * 16 + k
            total = total + columns[0:64, at : at + 1] * rows[at : at + 1]
            total = total + columns[64:128, at : at + 1] * other[at : at + 1]
        d_spec[k] = total
    sums = sums_ref[...].reshape(64, 128)
    d_local[...] = sums[:, 0:64]
    d_bias[...] = sums[0:1, 64:128]


def weights_call(modes_g, own_modes, scales, sums):
    vmem = pl.BlockSpec(memory_space=pltpu.VMEM)
    return pl.pallas_call(
        weights_kernel,
        out_shape=(
            jax.ShapeDtypeStruct((16, 64, 128), F32),
            jax.ShapeDtypeStruct((64, 64), F32),
            jax.ShapeDtypeStruct((1, 64), F32),
        ),
        in_specs=[vmem] * 4,
        out_specs=(vmem,) * 3,
    )(modes_g, own_modes, scales, sums)


def shards(base_field, cotangent, w_spec, w_local, bias, direction, shift):
    number = lax.axis_index("grp") + 1
    gray_code = jnp.bitwise_xor(number, number >> 1)
    picked = [
        jnp.where(gray_code >> bit_pos & 1 == 1, direction[:, bit_pos], 0)
        for bit_pos in range(BITS)
    ]
    mixed_bits = reduce(jnp.bitwise_xor, picked)
    sobol_point = jnp.bitwise_xor(mixed_bits, shift[0]).astype(F32) * 2.0 ** (-30)
    scale = 0.5 + sobol_point
    scale_rows = jnp.broadcast_to(jnp.concatenate([scale, scale])[None, :], (8, 128))
    grid_modes, own_modes, scales, kron = spectral_call(
        base_field, w_spec.reshape(16, 64, 128), w_local, scale_rows
    )
    output, cotan_pre, sums = cells_call(
        grid_modes, kron, bias, scale_rows, base_field, cotangent[0]
    )
    modes_g, total = gradient_call(cotan_pre, sums)
    d_spec, d_local, d_bias = weights_call(modes_g, own_modes, scales, total)
    return (output[None], d_spec.reshape(4, 4, 64, 128), d_local, d_bias.reshape(64))


def solution(mesh):
    return jax.shard_map(
        shards,
        mesh=mesh,
        in_specs=(
            P(None, "slab", None, None),
            P("grp", None, "slab", None, None),
            P("grp", "slab", None, None),
            P(),
            P(),
            P(),
            P("grp", None),
        ),
        out_specs=(P("grp", None, "slab", None, None), P("grp", "slab", None, None), P(), P()),
        check_vma=False,
    )
```

time: 211 us -> 91.8 us (0.44)
  Pallas kernels: 0 us -> 77.5 us
  blocking collectives: 74.5 us -> 0 us
  matrix products: 39.9 us -> 0 us
  starting transfers between devices: 28.7 us -> 0 us
  waiting for transfers between devices: 16.7 us -> 0 us
  between operations: 14.5 us -> 0.76 us
  local copies, waits for them, and re-layouts: 25 us -> 11.9 us
  other arithmetic: 11.2 us -> 1.2 us
    pallas_call x0 -> x4, Pallas kernels: none -> 77.5 us  [the longest x1 29.7 us: spectral_call(): pl.pallas_call(spectral_kernel, out_shape=(jax.ShapeDtypeStruct((64, 8, 1...]
    psum x1 -> x0, blocking collectives: 74.5 us -> none  [shards(): d_local, d_bias = lax.psum((local_grad, bias_grad), ('grp', 'slab'))]
    dot_general x19 -> x0, matrix products: 39.9 us -> none  [the longest x1 13.5 us: synth_yz(): jnp.einsum('xykrc,krz->cxyz', stacked, inverse_z, preferred_element_type=...]
    all_to_all x3 -> x0, starting transfers between devices: 28.4 us -> none  [the longest x2 20.4 us: analyse(): lax.all_to_all(slab_modes, 'slab', split_axis=1, concat_axis=0, tiled=True)]
    all_to_all x3 -> x0, waiting for transfers between devices: 15.9 us -> none  [the longest x2 13.1 us: analyse(): lax.all_to_all(slab_modes, 'slab', split_axis=1, concat_axis=0, tiled=True)]
    unnamed x20 -> x38, local copies, waits for them, and re-layouts: 19.9 us -> 11.9 us
    convert_element_type x3 -> x0, other arithmetic: 5.41 us -> none  [the longest x1 3.53 us: shards(): (base_field.astype(jnp.float32) * (0.5 + sobol_point)[:, None, None, None...]
    another operation x12 -> x0, other arithmetic: 2.56 us -> none
  transfers between devices with their start and end apart: 5 -> 0, of which waited for: 3 -> 0; matrix products, arithmetic and copies ran while one was open for 18% -> 0% of each run, Pallas kernels for 0% -> 0%
where the time goes in v1:
time: 91.8 us; the launch traced here: 91.3 us
  Pallas kernels  77.5 us (84%)
  local copies, waits for them, and re-layouts  11.9 us (13%)
  other arithmetic  1.2 us (1%)
    pallas_call x1, Pallas kernels, spectral_call(): pl.pallas_call(spectral_kernel, out_shape=(jax.ShapeDtypeStruct((64, 8, 1...  29.7 us
    pallas_call x1, Pallas kernels, cells_call(): pl.pallas_call(cells_kernel, grid=(8,), out_shape=(jax.ShapeDtypeStruct((...  25.7 us
    pallas_call x1, Pallas kernels, gradient_call(): pl.pallas_call(gradient_kernel, out_shape=(jax.ShapeDtypeStruct((4, 16, 1...  19.2 us
    unnamed x38, local copies, waits for them, and re-layouts  11.9 us
    pallas_call x1, Pallas kernels, weights_call(): pl.pallas_call(weights_kernel, out_shape=(jax.ShapeDtypeStruct((16, 64, 1...  2.96 us

profile of v1, /device:TPU:1, one launch (start us, length us, event | category | flops | bytes accessed | tf_op | source)
XLA Modules:
  0.0 91.3 jit_solution(10525317697900690278)
XLA Ops:
  0.6 0.0 copy-start.17
  0.6 0.0 copy-start.18
  0.7 1.1 %multiply_add_fusion = f32[64]{0:T(128)S(1)} fusion(s32[1,64]{1,0:T(1,128)} %param.22, s32[64,30]{0,1:T(8,128)} %param.21, pred[]{:T(512)S(6)} %eq.119, pred[]{:T(512)S(6)} %eq.118, pred[]{:T(512)S(6)} %eq.117, pred[]{:T(512)S(6)} %eq.116, pred[]{:T(512)S(6)} %eq.115, pred[]{:T(512)S(6)} %eq.114, pred[]{:T(512)S(6)} %eq.113, pred[]{:T(512)S(6)} %eq.112, ...), kind=kLoop, calls=%fused_computation.75 | loop fusion | flops 4032 | bytes 8222 | tf_op jit(solution)/shard_map/add | solution.py:658
  1.8 0.1 pad_maximum_fusion
  1.9 2.2 %copy-done = bf16[64,2,128,128]{3,2,1,0:T(8,128)(2,1)S(1)} copy-done((bf16[64,2,128,128]{3,2,1,0:T(8,128)(2,1)S(1)}, bf16[64,2,128,128]{3,2,1,0:T(8,128)(2,1)}, u32[]{:S(2)}) %copy-start) | copy-done | bytes 4194328
  4.1 0.9 copy-done.2
  5.0 0.9 %copy-done.4 = bf16[4,4,64,128]{3,2,1,0:T(8,128)(2,1)S(1)} copy-done((bf16[4,4,64,128]{3,2,1,0:T(8,128)(2,1)S(1)}, bf16[4,4,64,128]{3,2,1,0:T(8,128)(2,1)}, u32[]{:S(2)}) %copy-start.4) | copy-done | bytes 262168
  6.0 0.8 copy-done.5
  6.7 0.9 copy-done.7
  7.6 0.8 copy-done.9
  8.5 0.7 copy-done.11
  9.2 29.7 %shard_map.183 = (bf16[64,8,128]{2,1,0:T(8,128)(2,1)S(1)}, f32[16,128]{1,0:T(8,128)S(1)}, f32[4,8,128]{2,1,0:T(8,128)S(1)}, bf16[512,512]{1,0:T(8,128)(2,1)S(1)}) custom-call(bf16[64,2,128,128]{3,2,1,0:T(8,128)(2,1)S(1)} %copy-done, bf16[16,64,128]{2,1,0:T(8,128)(2,1)S(1)} %bitcast.151, bf16[64,64]{1,0:T(8,128)(2,1)S(1)} %copy-done.11, ...), custom_call_target="tpu_custom_call" | custom-call | tf_op jit(solution)/shard_map/pallas_call | solution.py:306
  38.9 0.0 copy-start.12
  38.9 0.6 copy-done.12
  39.5 0.6 copy-done.14
  40.1 0.0 copy-start.15
  40.1 2.2 %copy-done.15 = bf16[1,64,2,128,128]{4,3,2,1,0:T(8,128)(2,1)S(1)} copy-done((bf16[1,64,2,128,128]{4,3,2,1,0:T(8,128)(2,1)S(1)}, bf16[1,64,2,128,128]{4,3,2,1,0:T(8,128)(2,1)}, u32[]{:S(2)}) %copy-start.15) | copy-done | bytes 4194328
  42.3 25.7 %shard_map.184 = (bf16[64,2,128,128]{3,2,1,0:T(8,128)(2,1)}, bf16[64,2,128,128]{3,2,1,0:T(8,128)(2,1)S(1)}, f32[8,8,128]{2,1,0:T(8,128)S(1)}) custom-call(bf16[64,8,128]{2,1,0:T(8,128)(2,1)S(1)} %get-tuple-element.16.grid_modes, bf16[512,512]{1,0:T(8,128)(2,1)S(1)} %get-tuple-element.17.kron_ref, f32[64]{0:T(128)S(1)} %copy-done.16, ...), custom_call_target="tpu_custom_call" | custom-call | flops 4294967296 | bytes 16777216 | tf_op jit(solution)/shard_map/pallas_call | solution.py:462
  68.0 0.0 copy-done.3
  68.0 0.0 copy-done.8
  68.0 19.2 %shard_map.185 = (bf16[4,16,128]{2,1,0:T(8,128)(2,1)S(1)}, f32[8,8,128]{2,1,0:T(8,128)S(1)}) custom-call(bf16[64,2,128,128]{3,2,1,0:T(8,128)(2,1)S(1)} %get-tuple-element.19.cotan, f32[8,8,128]{2,1,0:T(8,128)S(1)} %get-tuple-element.20.sums_ref, bf16[64,256]{1,0:T(8,128)(2,1)S(1)} %copy-done.6, bf16[64,512]{1,0:T(8,128)(2,1)S(1)} %copy-done.8, ...), custom_call_target="tpu_custom_call" | custom-call | tf_op jit(solution)/shard_map/pallas_call | solution.py:587
  87.2 0.6 copy-done.10
  87.8 0.6 copy-done.13
  88.4 3.0 %shard_map.186 = (f32[16,64,128]{2,1,0:T(8,128)}, f32[64,64]{1,0:T(8,128)}, f32[1,64]{1,0:T(1,128)}) custom-call(bf16[4,16,128]{2,1,0:T(8,128)(2,1)} %copy-done.13, f32[16,128]{1,0:T(8,128)} %copy-done.14, f32[4,8,128]{2,1,0:T(8,128)} %copy-done.12, f32[8,8,128]{2,1,0:T(8,128)} %copy-done.10), custom_call_target="tpu_custom_call" | custom-call | tf_op jit(solution)/shard_map/pallas_call | solution.py:637
  (21 shorter events, 0.0 us)
Async XLA Ops:
  0.6 39.4 %copy-start.17 = (bf16[64,512]{1,0:T(8,128)(2,1)S(1)}, bf16[64,512]{1,0:T(8,128)(2,1)}, u32[]{:S(2)}) copy-start(bf16[64,512]{1,0:T(8,128)(2,1)} %constant.89.clone.ez_ref) | copy-start | bytes 196612
  0.6 39.4 %copy-start.18 = (bf16[256,64]{1,0:T(8,128)(2,1)S(1)}, bf16[256,64]{1,0:T(8,128)(2,1)}, u32[]{:S(2)}) copy-start(bf16[256,64]{1,0:T(8,128)(2,1)} %constant.88.clone.ey_ref) | copy-start | bytes 98308
  0.7 39.4 %copy-start.16 = (f32[64]{0:T(128)S(1)}, f32[64]{0:T(128)}, u32[]{:S(2)}) copy-start(f32[64]{0:T(128)} %bias_ref.1) | copy-start | bytes 772
  1.9 2.2 %copy-start = (bf16[64,2,128,128]{3,2,1,0:T(8,128)(2,1)S(1)}, bf16[64,2,128,128]{3,2,1,0:T(8,128)(2,1)}, u32[]{:S(2)}) copy-start(bf16[64,2,128,128]{3,2,1,0:T(8,128)(2,1)} %field_ref.1) | copy-start | bytes 12582916
  4.1 0.9 copy-start.2
  5.0 0.9 %copy-start.4 = (bf16[4,4,64,128]{3,2,1,0:T(8,128)(2,1)S(1)}, bf16[4,4,64,128]{3,2,1,0:T(8,128)(2,1)}, u32[]{:S(2)}) copy-start(bf16[4,4,64,128]{3,2,1,0:T(8,128)(2,1)} %param.18) | copy-start | bytes 786436
  6.0 0.8 copy-start.5
  6.7 0.9 copy-start.7
  7.6 0.8 copy-start.9
  8.5 0.7 copy-start.11
  9.2 30.9 %copy-start.1 = (bf16[64,2,128,128]{3,2,1,0:T(8,128)(2,1)S(1)}, bf16[64,2,128,128]{3,2,1,0:T(8,128)(2,1)}, u32[]{:S(2)}) copy-start(bf16[64,2,128,128]{3,2,1,0:T(8,128)(2,1)} %field_ref.1) | copy-start | bytes 12582916
  38.9 0.6 copy-start.12
  39.5 0.6 copy-start.14
  40.1 2.2 %copy-start.15 = (bf16[1,64,2,128,128]{4,3,2,1,0:T(8,128)(2,1)S(1)}, bf16[1,64,2,128,128]{4,3,2,1,0:T(8,128)(2,1)}, u32[]{:S(2)}) copy-start(bf16[1,64,2,128,128]{4,3,2,1,0:T(8,128)(2,1)} %param.17) | copy-start | bytes 12582916
  42.3 25.7 %copy-start.3 = (bf16[128,512]{1,0:T(8,128)(2,1)S(1)}, bf16[128,512]{1,0:T(8,128)(2,1)}, u32[]{:S(2)}) copy-start(bf16[128,512]{1,0:T(8,128)(2,1)} %constant.86.clone.tx_ref) | copy-start | bytes 393220
  42.3 25.7 %copy-start.6 = (bf16[64,256]{1,0:T(8,128)(2,1)S(1)}, bf16[64,256]{1,0:T(8,128)(2,1)}, u32[]{:S(2)}) copy-start(bf16[64,256]{1,0:T(8,128)(2,1)} %constant.84.clone.ty_ref) | copy-start | bytes 98308
  42.3 25.7 %copy-start.8 = (bf16[64,512]{1,0:T(8,128)(2,1)S(1)}, bf16[64,512]{1,0:T(8,128)(2,1)}, u32[]{:S(2)}) copy-start(bf16[64,512]{1,0:T(8,128)(2,1)} %constant.90.clone.zt_ref) | copy-start | bytes 196612
  87.2 0.6 copy-start.10
  87.8 0.6 copy-start.13

commit v2 on v1

v2 whole, which is shorter than its diff:
```python
from functools import reduce
import math

import jax
import jax.numpy as jnp
import ml_dtypes
import numpy as np
from jax import lax
from jax.experimental import pallas as pl
from jax.experimental.pallas import tpu as pltpu
from jax.sharding import PartitionSpec as P

CH = 64
NX = 128
NY = 128
NZ = 128
MODES = 16
BITS = 30
N_GRP = 4
N_SLAB = 64
N_LOW = 8
N_Z = 8
MESH = pl.DeviceIdType.MESH
F32 = jnp.float32
BF16 = jnp.bfloat16
MIB = 1024 * 1024


def waves(length, half):
    ids = np.arange(MODES)
    if not half:
        ids = np.where(ids < MODES // 2, ids, length - MODES + ids)
    angles = 2.0 * math.pi / length * (ids[:, None] * np.arange(length)[None, :] % length)
    return np.cos(angles), np.sin(angles)


def as_bf16(table):
    return np.asarray(table, np.float32).astype(ml_dtypes.bfloat16)


def table_ty():
    cos_y, sin_y = waves(NY, False)
    out = np.zeros((2, 2, MODES, 2, NY))
    for c2 in range(2):
        out[0, c2, :, c2] = cos_y
        out[1, c2, :, c2] = sin_y
    return as_bf16(out.reshape(64, 256))


def weights_z(backward):
    return np.where(np.arange(MODES) == 0, 1.0, 2.0 if backward else 1.0)[:, None]


def table_zt(backward):
    cos_z, sin_z = waves(NZ, True)
    weight = weights_z(backward)
    cos_z = (weight * cos_z).reshape(4, 4, NZ)
    sin_z = (weight * sin_z).reshape(4, 4, NZ)
    out = np.zeros((2, 4, 2, 4, 2, 2, NZ))
    for x in range(2):
        out[0, :, x, :, 0, x] = cos_z
        out[0, :, x, :, 1, x] = -sin_z
        out[1, :, x, :, 0, x] = -sin_z
        out[1, :, x, :, 1, x] = -cos_z
    return as_bf16(out.reshape(64, 512))


def table_tx():
    cos_x, sin_x = waves(NX, False)
    out = np.zeros((2, MODES, 4, NX, 4))
    for m in range(4):
        out[0, :, m, :, m] = cos_x
        out[1, :, m, :, m] = sin_x
    return as_bf16(out.reshape(128, 512))


def table_ey():
    cos_y, sin_y = waves(NY, False)
    out = np.zeros((2, NY, 2, 2, MODES))
    for c2 in range(2):
        out[c2, :, c2, 0] = cos_y.T
        out[c2, :, c2, 1] = -sin_y.T
    return as_bf16(out.reshape(256, 64))


def table_ez():
    cos_z, sin_z = waves(NZ, True)
    weight = weights_z(True) / math.sqrt(MODES**3)
    cos_z = (weight * cos_z).reshape(4, 4, NZ)
    sin_z = (weight * sin_z).reshape(4, 4, NZ)
    out = np.zeros((2, 4, 2, 4, 2, 2, NZ))
    for x in range(2):
        out[0, :, x, :, 0, x] = cos_z
        out[1, :, x, :, 0, x] = -sin_z
        out[0, :, x, :, 1, x] = sin_z
        out[1, :, x, :, 1, x] = cos_z
    return as_bf16(out.reshape(64, 512))


def lane_sign(rows, first, second):
    lane = lax.broadcasted_iota(jnp.int32, (rows, 128), 1)
    return jnp.where(lane < 64, first, second).astype(F32)


def turned(rows, first, second):
    return pltpu.roll(rows, 64, 1) * lane_sign(rows.shape[0], first, second)


def nt_dot(left, right, precision=None):
    return lax.dot_general(
        left, right, (((1,), (1,)), ((), ())), preferred_element_type=F32, precision=precision
    )


def fetch_field(field, held, sems):
    for part in range(8):
        rows = pl.ds(8 * part, 8)
        pltpu.make_async_copy(field.at[rows], held.at[rows], sems.at[part]).start()


def wait_field(field, held, sems, part):
    rows = pl.ds(8 * part, 8)
    pltpu.make_async_copy(field.at[rows], held.at[rows], sems.at[part]).wait()


def store_along_y(along_y, got, first):
    for cs in range(2):
        for c2 in range(2):
            at = cs * 32 + c2 * 16
            for x in range(2):
                start = (2 * cs + x) * 1024 + first + c2
                along_y[pl.ds(start, 16, stride=64), :] = got[
                    at : at + 16, x * 128 : x * 128 + 128
                ]


def along_z_modes(along_y, zt_ref, slab_modes):
    for quarter in range(4):
        rows = jnp.concatenate(
            [
                along_y[part * 1024 + quarter * 256 : part * 1024 + quarter * 256 + 256, :]
                for part in range(4)
            ],
            1,
        ).astype(BF16)
        got = nt_dot(zt_ref[...], rows)
        for jy in range(4):
            real = got[0:32, jy * 64 : jy * 64 + 64]
            imag = got[32:64, jy * 64 : jy * 64 + 64]
            owner = (quarter * 4 + jy) * 4
            slab_modes[owner : owner + 4] = (
                jnp.concatenate([real, imag], 1).reshape(4, 8, 128).astype(BF16)
            )


def greet(barrier, me, grp):
    def tell(step, carry):
        pl.semaphore_signal(
            barrier, inc=1, device_id={"slab": lax.rem(me + step, N_SLAB)}, device_id_type=MESH
        )
        return carry

    lax.fori_loop(1, N_SLAB, tell, 0)
    for step in range(1, N_GRP):
        pl.semaphore_signal(
            barrier, inc=1, device_id={"grp": lax.rem(grp + step, N_GRP)}, device_id_type=MESH
        )


def send_all(source, target, send_sem, recv_sem, me):
    low = lax.rem(me, N_LOW)
    z = me // N_LOW
    for dz in (4, 3, 5, 2, 6, 1, 7, 0):

        def go(step, carry):
            other = lax.rem(z + dz, N_Z) * N_LOW + lax.rem(low + step, N_LOW)
            pltpu.make_async_remote_copy(
                src_ref=source.at[other],
                dst_ref=target.at[me],
                send_sem=send_sem,
                recv_sem=recv_sem,
                device_id={"slab": other},
                device_id_type=MESH,
            ).start()
            return carry

        lax.fori_loop(1 if dz == 0 else 0, N_LOW, go, 0)
    target[pl.ds(me, 1)] = source[pl.ds(me, 1)]


def wait_blocks(source, target, send_sem, recv_sem, count, me):
    pltpu.make_async_remote_copy(
        src_ref=source.at[pl.ds(0, count)],
        dst_ref=target.at[pl.ds(0, count)],
        send_sem=send_sem,
        recv_sem=recv_sem,
        device_id={"slab": me},
        device_id_type=MESH,
    ).wait()


def send_grp(source, target, send_sem, recv_sem, grp, by_target):
    for step in range(1, N_GRP):
        other = lax.rem(grp + step, N_GRP)
        pltpu.make_async_remote_copy(
            src_ref=source.at[other] if by_target else source.at[grp],
            dst_ref=target.at[grp],
            send_sem=send_sem,
            recv_sem=recv_sem,
            device_id={"grp": other},
            device_id_type=MESH,
        ).start()


def x_modes(pencil, tx_ref):
    rows = pencil[...].astype(F32).reshape(512, 128).astype(BF16)
    both = jnp.dot(tx_ref[...], rows, preferred_element_type=F32)
    return both[:64] + turned(both[64:], 1.0, -1.0)


GELU_K = math.sqrt(2.0 / math.pi)
GELU_A = GELU_K * 0.044715
GRAD_SCALE = 1.0 / math.sqrt(N_GRP * NX * NY * NZ)


def local_step(part, held, kron, field_rows, local):
    y_at = pl.multiple_of(16 * part, 16)
    halves = [held[:, x, pl.ds(y_at, 16), :].astype(F32) for x in range(2)]
    for half in range(2):
        rows = jnp.concatenate(
            [block[:, 8 * half : 8 * half + 8].reshape(512, 128) for block in halves], 1
        ).astype(BF16)
        field_rows[part, :, half * 256 : half * 256 + 256] = rows
        got = jnp.dot(kron[...], rows, preferred_element_type=F32)
        local[:, pl.ds(pl.multiple_of(y_at + 8 * half, 8), 8), :] = got.reshape(64, 8, 256)


def fill_kron(wl_ref, scale_row, kron):
    local = (wl_ref[...].astype(F32) * scale_row[0:1, 0:64]).astype(BF16)
    pick = (
        lax.broadcasted_iota(jnp.int32, (64, 512), 0)
        == lax.broadcasted_iota(jnp.int32, (64, 512), 1) // 8
    )
    wide = jnp.dot(local, pick.astype(F32).astype(BF16), preferred_element_type=F32).astype(BF16)
    same = (
        lax.broadcasted_iota(jnp.int32, (64, 512), 0) % 8
        == lax.broadcasted_iota(jnp.int32, (64, 512), 1) % 8
    )
    row_ids = lax.broadcasted_iota(jnp.int32, (64, 64), 0) // 8
    col_ids = lax.broadcasted_iota(jnp.int32, (64, 64), 1)
    for octet in range(8):
        rows_of = (row_ids + 8 * octet == col_ids).astype(F32).astype(BF16)
        tall = jnp.dot(rows_of, wide, preferred_element_type=F32)
        kron[octet * 64 : octet * 64 + 64, :] = jnp.where(same, tall, 0.0).astype(BF16)


def fill_along_z(landed, ez_ref, along_z):
    for quarter in range(4):
        rows = landed[quarter * 16 : quarter * 16 + 16].astype(F32).reshape(128, 128)
        turn = rows.T
        per_c = jnp.concatenate(
            [
                jnp.concatenate(
                    [turn[0:64, jy * 32 : jy * 32 + 32], turn[64:128, jy * 32 : jy * 32 + 32]], 1
                )
                for jy in range(4)
            ],
            0,
        ).astype(BF16)
        got = jnp.dot(per_c, ez_ref[...], preferred_element_type=F32)
        for jy in range(4):
            for cs in range(2):
                for x in range(2):
                    start = x * 2048 + cs * 16 + quarter * 4 + jy
                    lane = cs * 256 + x * 128
                    along_z[pl.ds(start, 64, stride=32), :] = got[
                        jy * 64 : jy * 64 + 64, lane : lane + 128
                    ]


def cells_step(
    index, along_z, local, bias_ref, cotan_in, ey_ref, ty_ref, out_held, cotan_rows, bias_sum, along_y
):
    rows = jnp.concatenate(
        [along_z[pl.ds(pl.multiple_of(x * 2048 + 64 * index, 64), 64), :] for x in range(2)], 1
    ).astype(BF16)
    got = jnp.dot(ey_ref[...], rows, preferred_element_type=F32)
    cells = []
    for c2 in range(2):
        channel = 2 * index + c2
        both = []
        for x in range(2):
            lanes = slice(x * 128, x * 128 + 128)
            pre = got[c2 * 128 : c2 * 128 + 128, lanes] + (
                local[channel, :, lanes] + bias_ref[channel]
            )
            square = pre * pre
            half_tanh = 0.5 + 0.5 * jnp.tanh(pre * (GELU_K + GELU_A * square))
            out_held[channel, x] = (pre * half_tanh).astype(BF16)
            slope = half_tanh + half_tanh * (1.0 - half_tanh) * (
                pre * (2.0 * GELU_K + 6.0 * GELU_A * square)
            )
            both.append(slope * (cotan_in[channel, x].astype(F32) * GRAD_SCALE))
        total = both[0] + both[1]
        bias_sum[channel] = jnp.sum(total.reshape(16, 8, 128), axis=0)
        cells.append(both)
    for y8 in range(16):
        for x in range(2):
            block = jnp.concatenate(
                [cells[c2][x][8 * y8 : 8 * y8 + 8] for c2 in range(2)], 0
            ).astype(BF16)
            lane = (y8 % 2) * 256 + x * 128
            cotan_rows[
                y8 // 2, pl.ds(pl.multiple_of(16 * index, 16), 16), lane : lane + 128
            ] = block
    wide = jnp.concatenate([jnp.concatenate(both, 1) for both in cells], 0).astype(BF16)
    store_along_y(
        along_y, jnp.dot(ty_ref[...], wide, preferred_element_type=F32), 2 * index
    )


def sums_of(grad, bias_sum, scale_row):
    same = (
        lax.broadcasted_iota(jnp.int32, (512, 512), 0) % 8
        == lax.broadcasted_iota(jnp.int32, (512, 512), 1) % 8
    )
    per_c = jnp.sum(jnp.where(same, grad, 0.0).reshape(64, 8, 512), axis=1)
    pick = (
        lax.broadcasted_iota(jnp.int32, (512, 64), 0) // 8
        == lax.broadcasted_iota(jnp.int32, (512, 64), 1)
    ).astype(F32)
    d_local = jnp.dot(per_c, pick, preferred_element_type=F32, precision=lax.Precision.HIGHEST)
    d_local = d_local * scale_row[0:1, 0:64]
    lanes = jnp.sum(bias_sum[...], axis=1)
    d_bias = nt_dot(jnp.ones((8, 128), F32), lanes, lax.Precision.HIGHEST)
    side = jnp.concatenate([d_bias, jnp.zeros((56, 64), F32)], 0)
    return jnp.concatenate([d_local, side], 1).reshape(8, 8, 128)


def layer_kernel(
    field, cotan, w_hbm, wl_hbm, scale_hbm, bias_ref,
    ty_hbm, ztf_hbm, ztb_hbm, tx_hbm, txb_hbm, ey_hbm, ez_hbm,
    out_hbm, modes_out, own_modes, scales, sums_out,
    ty_ref, ztf_ref, ztb_ref, tx_ref, txb_ref, ey_ref, ez_ref, w_ref, wl_ref, scale_ref,
    held, cotan_in, out_held, field_rows, cotan_rows, local, along_y, along_z, kron, w_two,
    slab_modes, pencil, mixed, gathered, back, landed, slab_g, pencil_g, mixed_g, gathered_g,
    all_modes, scale_own, scale_all, bias_sum, own_sums, first, second, second_own, third,
    field_sems, cotan_sems, table_sems, out_sems, send_sems, recv_sems,
):
    me = lax.axis_index("slab")
    grp = lax.axis_index("grp")
    low = lax.rem(me, N_LOW)
    z = me // N_LOW
    barrier = pltpu.get_barrier_semaphore()
    small = [
        (ty_hbm, ty_ref), (ztf_hbm, ztf_ref), (scale_hbm, scale_ref), (wl_hbm, wl_ref),
        (w_hbm, w_ref), (tx_hbm, tx_ref), (txb_hbm, txb_ref), (ey_hbm, ey_ref),
        (ez_hbm, ez_ref), (ztb_hbm, ztb_ref),
    ]
    copies = [
        pltpu.make_async_copy(source, target, table_sems.at[at])
        for at, (source, target) in enumerate(small)
    ]
    for copy in copies[:2]:
        copy.start()
    fetch_field(field, held, field_sems)
    for copy in copies[2:]:
        copy.start()
    fetch_field(cotan, cotan_in, cotan_sems)
    greet(barrier, me, grp)
    for g_step in range(1, N_GRP):

        def tell(step, carry):
            pl.semaphore_signal(
                barrier,
                inc=1,
                device_id={
                    "grp": lax.rem(grp + g_step, N_GRP),
                    "slab": lax.rem(z + step, N_Z) * N_LOW + low,
                },
                device_id_type=MESH,
            )
            return carry

        lax.fori_loop(1, N_Z, tell, 0)

    copies[0].wait()

    def channels(part, carry):
        wait_field(field, held, field_sems, part)
        for pair in range(4):
            first_c = 8 * part + 2 * pair
            rows = jnp.concatenate(
                [
                    jnp.concatenate([held[first_c + c2, 0], held[first_c + c2, 1]], 1)
                    for c2 in range(2)
                ],
                0,
            )
            store_along_y(
                along_y, jnp.dot(ty_ref[...], rows, preferred_element_type=F32), first_c
            )
        return carry

    lax.fori_loop(0, 8, channels, 0)
    copies[1].wait()
    along_z_modes(along_y, ztf_ref, slab_modes)
    copies[2].wait()
    scale_own[grp] = scale_ref[...]
    scale_all[grp] = scale_ref[...]
    pl.semaphore_wait(barrier, N_SLAB - 1 + N_GRP - 1 + (N_GRP - 1) * (N_Z - 1))
    send_all(slab_modes, pencil, send_sems.at[0], recv_sems.at[0], me)
    send_grp(scale_own, scale_all, send_sems.at[1], recv_sems.at[1], grp, False)

    copies[3].wait()
    copies[4].wait()
    for k in range(16):
        block = w_ref[k].astype(F32)
        w_two[k * 128 : k * 128 + 64, :] = w_ref[k]
        w_two[k * 128 + 64 : k * 128 + 128, :] = turned(block, -1.0, 1.0).astype(BF16)
    fill_kron(wl_ref, scale_ref[...], kron)

    def local_some(part, carry):
        local_step(part, held, kron, field_rows, local)
        return carry

    lax.fori_loop(0, 3, local_some, 0)
    pltpu.make_async_remote_copy(
        src_ref=scale_own.at[pl.ds(0, N_GRP - 1)],
        dst_ref=scale_all.at[pl.ds(0, N_GRP - 1)],
        send_sem=send_sems.at[1],
        recv_sem=recv_sems.at[1],
        device_id={"slab": me},
        device_id_type=MESH,
    ).wait()
    scales[...] = scale_all[...]
    copies[5].wait()
    copies[6].wait()
    wait_blocks(slab_modes, pencil, send_sems.at[0], recv_sems.at[0], N_SLAB - 1, me)

    all_modes[...] = x_modes(pencil, tx_ref) * (1.0 / math.sqrt(NX * NY * NZ))
    own = all_modes[pl.ds(pl.multiple_of(16 * grp, 16), 16), :]
    own_modes[...] = own
    shifted = jnp.concatenate([own * scale_all[s, 0:1, :] for s in range(N_GRP)], 0)
    row_mode = lax.broadcasted_iota(jnp.int32, (64, 128), 0) % 16
    spread = jnp.concatenate(
        [jnp.where(row_mode == k, shifted, 0.0).astype(BF16) for k in range(16)], 1
    )
    mixed[...] = (
        jnp.dot(spread, w_two[...], preferred_element_type=F32).astype(BF16).reshape(4, 16, 128)
    )
    send_grp(mixed, gathered, send_sems.at[2], recv_sems.at[2], grp, True)
    gathered[pl.ds(grp, 1)] = mixed[pl.ds(grp, 1)]
    lax.fori_loop(3, 5, local_some, 0)
    wait_blocks(mixed, gathered, send_sems.at[2], recv_sems.at[2], N_GRP - 1, me)
    full = gathered[...].reshape(64, 128)
    both = jnp.concatenate([full, turned(full.astype(F32), -1.0, 1.0).astype(BF16)], 0)
    back[...] = (
        jnp.dot(txb_ref[...], both, preferred_element_type=F32).reshape(64, 8, 128).astype(BF16)
    )
    send_all(back, landed, send_sems.at[3], recv_sems.at[3], me)
    lax.fori_loop(5, 8, local_some, 0)
    for copy in copies[7:]:
        copy.wait()
    for part in range(8):
        wait_field(cotan, cotan_in, cotan_sems, part)
    wait_blocks(back, landed, send_sems.at[3], recv_sems.at[3], N_SLAB - 1, me)

    fill_along_z(landed, ez_ref, along_z)

    def some_cells(part, carry):
        for pair in range(2):
            cells_step(
                2 * part + pair, along_z, local, bias_ref, cotan_in, ey_ref, ty_ref, out_held,
                cotan_rows, bias_sum, along_y,
            )
        return carry

    def cells_part(part, carry):
        lax.fori_loop(2 * part, 2 * part + 2, some_cells, 0)
        rows = pl.ds(8 * part, 8)
        pltpu.make_async_copy(out_held.at[rows], out_hbm.at[rows], out_sems.at[part]).start()
        return carry

    lax.fori_loop(0, 8, cells_part, 0)

    grad = jnp.zeros((512, 512), F32)
    for part in range(8):
        grad = grad + nt_dot(cotan_rows[part], field_rows[part])
    own_sums[...] = sums_of(grad, bias_sum, scale_ref[...])

    def scatter(step, carry):
        other = lax.rem(low + step, N_LOW)
        pltpu.make_async_remote_copy(
            src_ref=own_sums.at[other],
            dst_ref=first.at[low],
            send_sem=send_sems.at[4],
            recv_sem=recv_sems.at[4],
            device_id={"slab": z * N_LOW + other},
            device_id_type=MESH,
        ).start()
        return carry

    lax.fori_loop(1, N_LOW, scatter, 0)
    first[pl.ds(low, 1)] = own_sums[pl.ds(low, 1)]
    along_z_modes(along_y, ztb_ref, slab_g)
    send_all(slab_g, pencil_g, send_sems.at[5], recv_sems.at[5], me)
    wait_blocks(own_sums, first, send_sems.at[4], recv_sems.at[4], N_LOW - 1, me)
    part_sum = jnp.sum(first[...], axis=0, keepdims=True)
    mine = grp * N_Z + z
    second[pl.ds(mine, 1)] = part_sum
    second_own[...] = part_sum
    for g_step in (2, 1, 3, 0):

        def spread_sum(step, carry):
            pltpu.make_async_remote_copy(
                src_ref=second_own.at[0],
                dst_ref=second.at[mine],
                send_sem=send_sems.at[6],
                recv_sem=recv_sems.at[6],
                device_id={
                    "grp": lax.rem(grp + g_step, N_GRP),
                    "slab": lax.rem(z + step, N_Z) * N_LOW + low,
                },
                device_id_type=MESH,
            ).start()
            return carry

        lax.fori_loop(1 if g_step == 0 else 0, N_Z, spread_sum, 0)
    wait_blocks(slab_g, pencil_g, send_sems.at[5], recv_sems.at[5], N_SLAB - 1, me)
    mixed_g[...] = x_modes(pencil_g, tx_ref).astype(BF16).reshape(4, 16, 128)
    send_grp(mixed_g, gathered_g, send_sems.at[7], recv_sems.at[7], grp, True)
    gathered_g[pl.ds(grp, 1)] = mixed_g[pl.ds(grp, 1)]
    wait_blocks(second, second, send_sems.at[6], recv_sems.at[6], N_GRP * N_Z - 1, me)
    third[pl.ds(low, 1)] = jnp.sum(second[...], axis=0, keepdims=True)

    def collect(step, carry):
        pltpu.make_async_remote_copy(
            src_ref=third.at[low],
            dst_ref=third.at[low],
            send_sem=send_sems.at[8],
            recv_sem=recv_sems.at[8],
            device_id={"slab": z * N_LOW + lax.rem(low + step, N_LOW)},
            device_id_type=MESH,
        ).start()
        return carry

    lax.fori_loop(1, N_LOW, collect, 0)
    wait_blocks(mixed_g, gathered_g, send_sems.at[7], recv_sems.at[7], N_GRP - 1, me)
    modes_out[...] = gathered_g[...]
    for part in range(8):
        rows = pl.ds(8 * part, 8)
        pltpu.make_async_copy(out_held.at[rows], out_hbm.at[rows], out_sems.at[part]).wait()
    wait_blocks(third, third, send_sems.at[8], recv_sems.at[8], N_LOW - 1, me)
    sums_out[...] = third[...]


def layer_call(field, cotangent, w_spec, w_local, scale_rows, bias):
    vmem = pl.BlockSpec(memory_space=pltpu.VMEM)
    hbm = pl.BlockSpec(memory_space=pl.ANY)
    tables = (
        table_ty(), table_zt(False), table_zt(True), table_tx(),
        np.ascontiguousarray(table_tx().T), table_ey(), table_ez(),
    )
    cells = (64, 2, 128, 128)
    blocks = pltpu.VMEM((64, 8, 128), BF16)
    quads = pltpu.VMEM((4, 16, 128), BF16)
    return pl.pallas_call(
        layer_kernel,
        out_shape=(
            jax.ShapeDtypeStruct(cells, BF16),
            jax.ShapeDtypeStruct((4, 16, 128), BF16),
            jax.ShapeDtypeStruct((16, 128), F32),
            jax.ShapeDtypeStruct((4, 8, 128), F32),
            jax.ShapeDtypeStruct((8, 8, 128), F32),
        ),
        in_specs=[hbm] * 5 + [pl.BlockSpec(memory_space=pltpu.SMEM)] + [hbm] * 7,
        out_specs=(hbm,) + (vmem,) * 4,
        scratch_shapes=[pltpu.VMEM(table.shape, BF16) for table in tables]
        + [
            pltpu.VMEM((16, 64, 128), BF16),
            pltpu.VMEM((64, 64), BF16),
            pltpu.VMEM((8, 128), F32),
            pltpu.VMEM(cells, BF16),
            pltpu.VMEM(cells, BF16),
            pltpu.VMEM(cells, BF16),
            pltpu.VMEM((8, 512, 512), BF16),
            pltpu.VMEM((8, 512, 512), BF16),
            pltpu.VMEM((64, 128, 256), F32),
            pltpu.VMEM((4096, 128), F32),
            pltpu.VMEM((4096, 128), F32),
            pltpu.VMEM((512, 512), BF16),
            pltpu.VMEM((2048, 128), BF16),
            blocks, blocks, quads, quads, blocks, blocks, blocks, blocks, quads, quads,
            pltpu.VMEM((64, 128), F32),
            pltpu.VMEM((4, 8, 128), F32),
            pltpu.VMEM((4, 8, 128), F32),
            pltpu.VMEM((64, 8, 128), F32),
            pltpu.VMEM((8, 8, 128), F32),
            pltpu.VMEM((8, 8, 128), F32),
            pltpu.VMEM((32, 8, 128), F32),
            pltpu.VMEM((1, 8, 128), F32),
            pltpu.VMEM((8, 8, 128), F32),
            pltpu.SemaphoreType.DMA((8,)),
            pltpu.SemaphoreType.DMA((8,)),
            pltpu.SemaphoreType.DMA((10,)),
            pltpu.SemaphoreType.DMA((8,)),
            pltpu.SemaphoreType.DMA((9,)),
            pltpu.SemaphoreType.DMA((9,)),
        ],
        compiler_params=pltpu.CompilerParams(
            collective_id=0, has_side_effects=True, vmem_limit_bytes=58 * MIB
        ),
    )(field, cotangent, w_spec, w_local, scale_rows, bias, *tables)


def weights_kernel(
    out_hbm, modes_hbm, own_hbm, scales_hbm, sums_hbm,
    output, d_spec, d_local, d_bias,
    modes_g, own_modes, scales, sums_ref, sems,
):
    small = [
        (modes_hbm, modes_g), (own_hbm, own_modes), (scales_hbm, scales), (sums_hbm, sums_ref)
    ]
    copies = [
        pltpu.make_async_copy(source, target, sems.at[8 + at])
        for at, (source, target) in enumerate(small)
    ]
    for copy in copies:
        copy.start()
    moves = [
        pltpu.make_async_copy(
            out_hbm.at[pl.ds(8 * part, 8)], output.at[pl.ds(8 * part, 8)], sems.at[part]
        )
        for part in range(8)
    ]
    for move in moves:
        move.start()
    for copy in copies:
        copy.wait()
    own = own_modes[...]
    shifted = jnp.concatenate([own * scales[s, 0:1, :] for s in range(N_GRP)], 0)
    columns = shifted.T
    rows = modes_g[...].astype(F32).reshape(64, 128)
    other = turned(rows, 1.0, -1.0)
    for k in range(16):
        total = jnp.zeros((64, 128), F32)
        for s in range(N_GRP):
            at = s * 16 + k
            total = total + columns[0:64, at : at + 1] * rows[at : at + 1]
            total = total + columns[64:128, at : at + 1] * other[at : at + 1]
        d_spec[k] = total
    sums = sums_ref[...].reshape(64, 128)
    d_local[...] = sums[:, 0:64]
    d_bias[...] = sums[0:1, 64:128]
    for move in moves:
        move.wait()


def weights_call(out, modes_g, own_modes, scales, sums):
    vmem = pl.BlockSpec(memory_space=pltpu.VMEM)
    hbm = pl.BlockSpec(memory_space=pl.ANY)
    return pl.pallas_call(
        weights_kernel,
        out_shape=(
            jax.ShapeDtypeStruct(out.shape, BF16),
            jax.ShapeDtypeStruct((16, 64, 128), F32),
            jax.ShapeDtypeStruct((64, 64), F32),
            jax.ShapeDtypeStruct((1, 64), F32),
        ),
        in_specs=[hbm] * 5,
        out_specs=(hbm,) + (vmem,) * 3,
        scratch_shapes=[
            pltpu.VMEM((4, 16, 128), BF16),
            pltpu.VMEM((16, 128), F32),
            pltpu.VMEM((4, 8, 128), F32),
            pltpu.VMEM((8, 8, 128), F32),
            pltpu.SemaphoreType.DMA((12,)),
        ],
        compiler_params=pltpu.CompilerParams(vmem_limit_bytes=58 * MIB),
    )(out, modes_g, own_modes, scales, sums)


def shards(base_field, cotangent, w_spec, w_local, bias, direction, shift):
    number = lax.axis_index("grp") + 1
    gray_code = jnp.bitwise_xor(number, number >> 1)
    picked = [
        jnp.where(gray_code >> bit_pos & 1 == 1, direction[:, bit_pos], 0)
        for bit_pos in range(N_GRP.bit_length())
    ]
    mixed_bits = reduce(jnp.bitwise_xor, picked)
    sobol_point = jnp.bitwise_xor(mixed_bits, shift[0]).astype(F32) * 2.0 ** (-30)
    scale = 0.5 + sobol_point
    scale_rows = jnp.broadcast_to(jnp.concatenate([scale, scale])[None, :], (8, 128))
    out, modes_g, own_modes, scales, sums = layer_call(
        base_field, cotangent[0], w_spec.reshape(16, 64, 128), w_local, scale_rows, bias
    )
    output, d_spec, d_local, d_bias = weights_call(out, modes_g, own_modes, scales, sums)
    return (output[None], d_spec.reshape(4, 4, 64, 128), d_local, d_bias.reshape(64))


def solution(mesh):
    return jax.shard_map(
        shards,
        mesh=mesh,
        in_specs=(
            P(None, "slab", None, None),
            P("grp", None, "slab", None, None),
            P("grp", "slab", None, None),
            P(),
            P(),
            P(),
            P("grp", None),
        ),
        out_specs=(P("grp", None, "slab", None, None), P("grp", "slab", None, None), P(), P()),
        check_vma=False,
    )
```

time: 91.8 us -> 194 us (2.11)
  Pallas kernels: 77.5 us -> 192 us
  local copies, waits for them, and re-layouts: 11.9 us -> 0.6 us
    pallas_call x4 -> x2, Pallas kernels: 77.5 us -> 192 us  [the longest x1 129 us: weights_call(): pl.pallas_call(weights_kernel, out_shape=(jax.ShapeDtypeStruct(out.shape,...]
    unnamed x38 -> x0, local copies, waits for them, and re-layouts: 11.9 us -> none
where the time goes in v2:
time: 194 us
  Pallas kernels  192 us (99%)
    pallas_call x1, Pallas kernels, weights_call(): pl.pallas_call(weights_kernel, out_shape=(jax.ShapeDtypeStruct(out.shape,...  129 us
    pallas_call x1, Pallas kernels, layer_call(): pl.pallas_call(layer_kernel, out_shape=(jax.ShapeDtypeStruct(cells, BF16)...  62.9 us

profile of v2, /device:TPU:1, one launch (start us, length us, event | category | flops | bytes accessed | tf_op | source)
XLA Modules:
  0.0 194.1 jit_solution(4016153779976913506)
XLA Ops:
  0.6 0.8 fusion.4
  1.5 0.1 pad_maximum_fusion
  1.5 0.6 broadcast_in_dim.16.scale_hbm
  2.1 62.9 %shard_map.165 = (bf16[64,2,128,128]{3,2,1,0:T(8,128)(2,1)}, bf16[4,16,128]{2,1,0:T(8,128)(2,1)}, f32[16,128]{1,0:T(8,128)}, f32[4,8,128]{2,1,0:T(8,128)}, f32[8,8,128]{2,1,0:T(8,128)}) custom-call(bf16[64,2,128,128]{3,2,1,0:T(8,128)(2,1)} %field.1, bf16[64,2,128,128]{3,2,1,0:T(8,128)(2,1)} %bitcast.15, bf16[16,64,128]{2,1,0:T(8,128)(2,1)} %bitcast.16, ...), custom_call_target="tpu_custom_call" | custom-call | tf_op jit(solution)/shard_map/pallas_call | solution.py:568
  65.0 129.1 %shard_map.166 = (bf16[64,2,128,128]{3,2,1,0:T(8,128)(2,1)}, f32[16,64,128]{2,1,0:T(8,128)}, f32[64,64]{1,0:T(8,128)}, f32[1,64]{1,0:T(1,128)}) custom-call(bf16[64,2,128,128]{3,2,1,0:T(8,128)(2,1)} %get-tuple-element.13.out_hbm, bf16[4,16,128]{2,1,0:T(8,128)(2,1)} %get-tuple-element.14.modes_hbm, f32[16,128]{1,0:T(8,128)} %get-tuple-element.15.own_hbm, ...), custom_call_target="tpu_custom_call" | custom-call | tf_op jit(solution)/shard_map/pallas_call | solution.py:663

commit v3 on v2

--- a/solution.py
+++ b/solution.py
@@ -617,25 +617,25 @@
 def weights_kernel(
     out_hbm, modes_hbm, own_hbm, scales_hbm, sums_hbm,
     output, d_spec, d_local, d_bias,
-    modes_g, own_modes, scales, sums_ref, sems,
+    held, modes_g, own_modes, scales, sums_ref, sems, in_sems, out_sems,
 ):
     small = [
         (modes_hbm, modes_g), (own_hbm, own_modes), (scales_hbm, scales), (sums_hbm, sums_ref)
     ]
     copies = [
-        pltpu.make_async_copy(source, target, sems.at[8 + at])
+        pltpu.make_async_copy(source, target, sems.at[at])
         for at, (source, target) in enumerate(small)
     ]
     for copy in copies:
         copy.start()
-    moves = [
-        pltpu.make_async_copy(
-            out_hbm.at[pl.ds(8 * part, 8)], output.at[pl.ds(8 * part, 8)], sems.at[part]
-        )
-        for part in range(8)
-    ]
-    for move in moves:
-        move.start()
+    ins = []
+    outs = []
+    for part in range(8):
+        rows = pl.ds(8 * part, 8)
+        ins.append(pltpu.make_async_copy(out_hbm.at[rows], held.at[rows], in_sems.at[part]))
+        outs.append(pltpu.make_async_copy(held.at[rows], output.at[rows], out_sems.at[part]))
+    for copy in ins:
+        copy.start()
     for copy in copies:
         copy.wait()
     own = own_modes[...]
@@ -650,11 +650,14 @@
             total = total + columns[0:64, at : at + 1] * rows[at : at + 1]
             total = total + columns[64:128, at : at + 1] * other[at : at + 1]
         d_spec[k] = total
+        if k % 2:
+            ins[k // 2].wait()
+            outs[k // 2].start()
     sums = sums_ref[...].reshape(64, 128)
     d_local[...] = sums[:, 0:64]
     d_bias[...] = sums[0:1, 64:128]
-    for move in moves:
-        move.wait()
+    for copy in outs:
+        copy.wait()
 
 
 def weights_call(out, modes_g, own_modes, scales, sums):
@@ -671,11 +674,14 @@
         in_specs=[hbm] * 5,
         out_specs=(hbm,) + (vmem,) * 3,
         scratch_shapes=[
+            pltpu.VMEM(out.shape, BF16),
             pltpu.VMEM((4, 16, 128), BF16),
             pltpu.VMEM((16, 128), F32),
             pltpu.VMEM((4, 8, 128), F32),
             pltpu.VMEM((8, 8, 128), F32),
-            pltpu.SemaphoreType.DMA((12,)),
+            pltpu.SemaphoreType.DMA((4,)),
+            pltpu.SemaphoreType.DMA((8,)),
+            pltpu.SemaphoreType.DMA((8,)),
         ],
         compiler_params=pltpu.CompilerParams(vmem_limit_bytes=58 * MIB),
     )(out, modes_g, own_modes, scales, sums)

time: 194 us -> 70.6 us (0.36)
  Pallas kernels: 192 us -> 68.4 us
    pallas_call x1, Pallas kernels: 129 us -> 5.51 us  [weights_call(): pl.pallas_call(weights_kernel, out_shape=(jax.ShapeDtypeStruct(out.shape,...]
where the time goes in v3:
time: 70.6 us; the launch traced here: 70.5 us
  Pallas kernels  68.4 us (97%)
  other arithmetic  0.89 us (1%)
    pallas_call x1, Pallas kernels, layer_call(): pl.pallas_call(layer_kernel, out_shape=(jax.ShapeDtypeStruct(cells, BF16)...  62.9 us
    pallas_call x1, Pallas kernels, weights_call(): pl.pallas_call(weights_kernel, out_shape=(jax.ShapeDtypeStruct(out.shape,...  5.51 us

profile of v3, /device:TPU:1, one launch (start us, length us, event | category | flops | bytes accessed | tf_op | source)
XLA Modules:
  0.0 70.5 jit_solution(5421037142903234854)
XLA Ops:
  0.6 0.8 %fusion.4 = f32[64]{0:T(128)S(1)} fusion(s32[1,64]{1,0:T(1,128)} %param.20, s32[64,30]{0,1:T(8,128)} %param.19, pred[]{:T(512)S(6)} %eq.11, pred[]{:T(512)S(6)} %eq.10, pred[]{:T(512)S(6)} %eq.9), kind=kLoop, calls=%fused_computation.9 | loop fusion | flops 576 | bytes 1283 | tf_op jit(solution)/shard_map/add | solution.py:699
  1.5 0.1 pad_maximum_fusion
  1.5 0.6 broadcast_in_dim.16.scale_hbm
  2.1 62.9 %shard_map.165 = (bf16[64,2,128,128]{3,2,1,0:T(8,128)(2,1)}, bf16[4,16,128]{2,1,0:T(8,128)(2,1)}, f32[16,128]{1,0:T(8,128)}, f32[4,8,128]{2,1,0:T(8,128)}, f32[8,8,128]{2,1,0:T(8,128)}) custom-call(bf16[64,2,128,128]{3,2,1,0:T(8,128)(2,1)} %field.1, bf16[64,2,128,128]{3,2,1,0:T(8,128)(2,1)} %bitcast.15, bf16[16,64,128]{2,1,0:T(8,128)(2,1)} %bitcast.16, ...), custom_call_target="tpu_custom_call" | custom-call | tf_op jit(solution)/shard_map/pallas_call | solution.py:568
  65.0 5.5 %shard_map.166 = (bf16[64,2,128,128]{3,2,1,0:T(8,128)(2,1)}, f32[16,64,128]{2,1,0:T(8,128)}, f32[64,64]{1,0:T(8,128)}, f32[1,64]{1,0:T(1,128)}) custom-call(bf16[64,2,128,128]{3,2,1,0:T(8,128)(2,1)} %get-tuple-element.13.out_hbm, bf16[4,16,128]{2,1,0:T(8,128)(2,1)} %get-tuple-element.14.modes_hbm, f32[16,128]{1,0:T(8,128)} %get-tuple-element.15.own_hbm, ...), custom_call_target="tpu_custom_call" | custom-call | tf_op jit(solution)/shard_map/pallas_call | solution.py:666

commit v4 on v3

--- a/solution.py
+++ b/solution.py
@@ -1,4 +1,3 @@
-from functools import reduce
 import math
 
 import jax
@@ -24,6 +23,9 @@
 F32 = jnp.float32
 BF16 = jnp.bfloat16
 MIB = 1024 * 1024
+GELU_K = math.sqrt(2.0 / math.pi)
+GELU_A = 0.044715
+GRAD_SCALE = 1.0 / math.sqrt(N_GRP * NX * NY * NZ)
 
 
 def waves(length, half):
@@ -54,6 +56,8 @@
 def table_zt(backward):
     cos_z, sin_z = waves(NZ, True)
     weight = weights_z(backward)
+    if backward:
+        weight = weight * GRAD_SCALE
     cos_z = (weight * cos_z).reshape(4, 4, NZ)
     sin_z = (weight * sin_z).reshape(4, 4, NZ)
     out = np.zeros((2, 4, 2, 4, 2, 2, NZ))
@@ -218,12 +222,7 @@
     return both[:64] + turned(both[64:], 1.0, -1.0)
 
 
-GELU_K = math.sqrt(2.0 / math.pi)
-GELU_A = GELU_K * 0.044715
-GRAD_SCALE = 1.0 / math.sqrt(N_GRP * NX * NY * NZ)
-
-
-def local_step(part, held, kron, field_rows, local):
+def local_step(part, held, kron, bias_rows, field_rows, local):
     y_at = pl.multiple_of(16 * part, 16)
     halves = [held[:, x, pl.ds(y_at, 16), :].astype(F32) for x in range(2)]
     for half in range(2):
@@ -232,7 +231,24 @@
         ).astype(BF16)
         field_rows[part, :, half * 256 : half * 256 + 256] = rows
         got = jnp.dot(kron[...], rows, preferred_element_type=F32)
-        local[:, pl.ds(pl.multiple_of(y_at + 8 * half, 8), 8), :] = got.reshape(64, 8, 256)
+        added = bias_rows[...]
+        local[:, pl.ds(pl.multiple_of(y_at + 8 * half, 8), 8), :] = got.reshape(
+            64, 8, 256
+        ) + jnp.concatenate([added, added], 2)
+
+
+def scale_rows(grp, direction_ref, shift_ref):
+    number = grp + 1
+    gray_code = number ^ (number >> 1)
+    bits = jnp.zeros((64, 1), jnp.int32)
+    for bit_pos in range(N_GRP.bit_length()):
+        bits = bits ^ (direction_ref[:, bit_pos : bit_pos + 1] * ((gray_code >> bit_pos) & 1))
+    diagonal = lax.broadcasted_iota(jnp.int32, (64, 64), 0) == lax.broadcasted_iota(
+        jnp.int32, (64, 64), 1
+    )
+    row = jnp.sum(jnp.where(diagonal, jnp.broadcast_to(bits, (64, 64)), 0), axis=0, keepdims=True)
+    scale = 0.5 + (row ^ shift_ref[...]).astype(F32) * 2.0 ** (-BITS)
+    return jnp.broadcast_to(jnp.concatenate([scale, scale], 1), (8, 128))
 
 
 def fill_kron(wl_ref, scale_row, kron):
@@ -278,45 +294,63 @@
                     ]
 
 
-def cells_step(
-    index, along_z, local, bias_ref, cotan_in, ey_ref, ty_ref, out_held, cotan_rows, bias_sum, along_y
-):
+def synthesis(group, along_z, local, ey_ref, pre_act):
     rows = jnp.concatenate(
-        [along_z[pl.ds(pl.multiple_of(x * 2048 + 64 * index, 64), 64), :] for x in range(2)], 1
-    ).astype(BF16)
+        [
+            along_z[pl.ds(x * 2048 + 256 * group + 64 * pair, 64), :].astype(BF16)
+            for pair in range(4)
+            for x in range(2)
+        ],
+        1,
+    )
     got = jnp.dot(ey_ref[...], rows, preferred_element_type=F32)
-    cells = []
-    for c2 in range(2):
-        channel = 2 * index + c2
-        both = []
+    for pair in range(4):
+        for c2 in range(2):
+            at = slice(c2 * 128, c2 * 128 + 128)
+            lanes = slice(pair * 256, pair * 256 + 256)
+            pre_act[at, lanes] = (
+                got[at, lanes] + local[8 * group + 2 * pair + c2]
+            ).astype(BF16)
+
+
+def activation(group, pre_act, cotan_in, out_held, cotan_pre):
+    for pair in range(4):
+        for c2 in range(2):
+            for x in range(2):
+                channel = 8 * group + 2 * pair + c2
+                at = slice(c2 * 128, c2 * 128 + 128)
+                lanes = slice(pair * 256 + x * 128, pair * 256 + x * 128 + 128)
+                pre = pre_act[at, lanes]
+                square = pre * pre
+                inner = pre * (1.0 + GELU_A * square)
+                tanh = jnp.tanh(inner.astype(F32) * GELU_K)
+                half = 0.5 + 0.5 * tanh
+                bell = (half * (GELU_K - GELU_K * tanh)).astype(BF16)
+                half = half.astype(BF16)
+                out_held[channel, x] = pre * half
+                slope = half + bell * (pre * (1.0 + (3.0 * GELU_A) * square))
+                cotan_pre[at, lanes] = slope * cotan_in[channel, x]
+
+
+def gradient_modes(group, cotan_pre, ty_ref, cotan_rows, bias_sum, along_y):
+    got = jnp.dot(ty_ref[...], cotan_pre[...], preferred_element_type=F32)
+    for pair in range(4):
+        store_along_y(along_y, got[:, pair * 256 : pair * 256 + 256], 8 * group + 2 * pair)
+    for pair in range(4):
         for x in range(2):
-            lanes = slice(x * 128, x * 128 + 128)
-            pre = got[c2 * 128 : c2 * 128 + 128, lanes] + (
-                local[channel, :, lanes] + bias_ref[channel]
-            )
-            square = pre * pre
-            half_tanh = 0.5 + 0.5 * jnp.tanh(pre * (GELU_K + GELU_A * square))
-            out_held[channel, x] = (pre * half_tanh).astype(BF16)
-            slope = half_tanh + half_tanh * (1.0 - half_tanh) * (
-                pre * (2.0 * GELU_K + 6.0 * GELU_A * square)
-            )
-            both.append(slope * (cotan_in[channel, x].astype(F32) * GRAD_SCALE))
-        total = both[0] + both[1]
-        bias_sum[channel] = jnp.sum(total.reshape(16, 8, 128), axis=0)
-        cells.append(both)
-    for y8 in range(16):
-        for x in range(2):
-            block = jnp.concatenate(
-                [cells[c2][x][8 * y8 : 8 * y8 + 8] for c2 in range(2)], 0
-            ).astype(BF16)
-            lane = (y8 % 2) * 256 + x * 128
-            cotan_rows[
-                y8 // 2, pl.ds(pl.multiple_of(16 * index, 16), 16), lane : lane + 128
-            ] = block
-    wide = jnp.concatenate([jnp.concatenate(both, 1) for both in cells], 0).astype(BF16)
-    store_along_y(
-        along_y, jnp.dot(ty_ref[...], wide, preferred_element_type=F32), 2 * index
-    )
+            lanes = slice(pair * 256 + x * 128, pair * 256 + x * 128 + 128)
+            wide = cotan_pre[:, lanes].astype(F32)
+            sums = jnp.sum(wide.reshape(2, 16, 8, 128), axis=1)
+            for c2 in range(2):
+                bias_sum[8 * group + 2 * pair + c2, x * 8 : x * 8 + 8] = sums[c2]
+            for y8 in range(16):
+                block = jnp.concatenate(
+                    [wide[c2 * 128 + 8 * y8 : c2 * 128 + 8 * y8 + 8] for c2 in range(2)], 0
+                )
+                lane = (y8 % 2) * 256 + x * 128
+                cotan_rows[
+                    y8 // 2, pl.ds(64 * group + 16 * pair, 16), lane : lane + 128
+                ] = block.astype(BF16)
 
 
 def sums_of(grad, bias_sum, scale_row):
@@ -330,21 +364,35 @@
         == lax.broadcasted_iota(jnp.int32, (512, 64), 1)
     ).astype(F32)
     d_local = jnp.dot(per_c, pick, preferred_element_type=F32, precision=lax.Precision.HIGHEST)
-    d_local = d_local * scale_row[0:1, 0:64]
+    d_local = d_local * (scale_row[0:1, 0:64] * GRAD_SCALE)
     lanes = jnp.sum(bias_sum[...], axis=1)
-    d_bias = nt_dot(jnp.ones((8, 128), F32), lanes, lax.Precision.HIGHEST)
+    d_bias = nt_dot(jnp.full((8, 128), GRAD_SCALE, F32), lanes, lax.Precision.HIGHEST)
     side = jnp.concatenate([d_bias, jnp.zeros((56, 64), F32)], 0)
     return jnp.concatenate([d_local, side], 1).reshape(8, 8, 128)
 
 
+def weight_terms(gathered_g, shifted_modes, d_spec):
+    columns = shifted_modes[...].T
+    rows = gathered_g[...].astype(F32).reshape(64, 128)
+    other = turned(rows, 1.0, -1.0)
+    for k in range(16):
+        total = jnp.zeros((64, 128), F32)
+        for s in range(N_GRP):
+            at = s * 16 + k
+            total = total + columns[0:64, at : at + 1] * rows[at : at + 1]
+            total = total + columns[64:128, at : at + 1] * other[at : at + 1]
+        d_spec[k] = total
+
+
 def layer_kernel(
-    field, cotan, w_hbm, wl_hbm, scale_hbm, bias_ref,
+    field, cotan, w_hbm, wl_hbm, direction_hbm, shift_hbm, bias_ref,
     ty_hbm, ztf_hbm, ztb_hbm, tx_hbm, txb_hbm, ey_hbm, ez_hbm,
-    out_hbm, modes_out, own_modes, scales, sums_out,
-    ty_ref, ztf_ref, ztb_ref, tx_ref, txb_ref, ey_ref, ez_ref, w_ref, wl_ref, scale_ref,
+    out_hbm, spec_hbm, sums_out,
+    ty_ref, ztf_ref, ztb_ref, tx_ref, txb_ref, ey_ref, ez_ref, w_ref, wl_ref, direction_ref, shift_ref, scale_ref,
     held, cotan_in, out_held, field_rows, cotan_rows, local, along_y, along_z, kron, w_two,
+    d_spec, pre_even, pre_odd, cotan_even, cotan_odd, bias_rows,
     slab_modes, pencil, mixed, gathered, back, landed, slab_g, pencil_g, mixed_g, gathered_g,
-    all_modes, scale_own, scale_all, bias_sum, own_sums, first, second, second_own, third,
+    all_modes, shifted_modes, scale_own, scale_all, bias_sum, own_sums, first, second, second_own, third,
     field_sems, cotan_sems, table_sems, out_sems, send_sems, recv_sems,
 ):
     me = lax.axis_index("slab")
@@ -353,9 +401,9 @@
     z = me // N_LOW
     barrier = pltpu.get_barrier_semaphore()
     small = [
-        (ty_hbm, ty_ref), (ztf_hbm, ztf_ref), (scale_hbm, scale_ref), (wl_hbm, wl_ref),
+        (ty_hbm, ty_ref), (ztf_hbm, ztf_ref), (direction_hbm, direction_ref), (wl_hbm, wl_ref),
         (w_hbm, w_ref), (tx_hbm, tx_ref), (txb_hbm, txb_ref), (ey_hbm, ey_ref),
-        (ez_hbm, ez_ref), (ztb_hbm, ztb_ref),
+        (ez_hbm, ez_ref), (ztb_hbm, ztb_ref), (shift_hbm, shift_ref),
     ]
     copies = [
         pltpu.make_async_copy(source, target, table_sems.at[at])
@@ -386,26 +434,24 @@
 
     copies[0].wait()
 
-    def channels(part, carry):
+    for part in range(8):
         wait_field(field, held, field_sems, part)
+        rows = jnp.concatenate(
+            [
+                jnp.concatenate([held[8 * part + 2 * pair + c2, x] for c2 in range(2)], 0)
+                for pair in range(4)
+                for x in range(2)
+            ],
+            1,
+        )
+        got = jnp.dot(ty_ref[...], rows, preferred_element_type=F32)
         for pair in range(4):
-            first_c = 8 * part + 2 * pair
-            rows = jnp.concatenate(
-                [
-                    jnp.concatenate([held[first_c + c2, 0], held[first_c + c2, 1]], 1)
-                    for c2 in range(2)
-                ],
-                0,
-            )
-            store_along_y(
-                along_y, jnp.dot(ty_ref[...], rows, preferred_element_type=F32), first_c
-            )
-        return carry
-
-    lax.fori_loop(0, 8, channels, 0)
+            store_along_y(along_y, got[:, pair * 256 : pair * 256 + 256], 8 * part + 2 * pair)
     copies[1].wait()
     along_z_modes(along_y, ztf_ref, slab_modes)
     copies[2].wait()
+    copies[10].wait()
+    scale_ref[...] = scale_rows(grp, direction_ref, shift_ref)
     scale_own[grp] = scale_ref[...]
     scale_all[grp] = scale_ref[...]
     pl.semaphore_wait(barrier, N_SLAB - 1 + N_GRP - 1 + (N_GRP - 1) * (N_Z - 1))
@@ -419,9 +465,11 @@
         w_two[k * 128 : k * 128 + 64, :] = w_ref[k]
         w_two[k * 128 + 64 : k * 128 + 128, :] = turned(block, -1.0, 1.0).astype(BF16)
     fill_kron(wl_ref, scale_ref[...], kron)
+    for channel in range(CH):
+        bias_rows[channel] = jnp.full((8, 128), bias_ref[channel], F32)
 
     def local_some(part, carry):
-        local_step(part, held, kron, field_rows, local)
+        local_step(part, held, kron, bias_rows, field_rows, local)
         return carry
 
     lax.fori_loop(0, 3, local_some, 0)
@@ -433,15 +481,14 @@
         device_id={"slab": me},
         device_id_type=MESH,
     ).wait()
-    scales[...] = scale_all[...]
     copies[5].wait()
     copies[6].wait()
     wait_blocks(slab_modes, pencil, send_sems.at[0], recv_sems.at[0], N_SLAB - 1, me)
 
     all_modes[...] = x_modes(pencil, tx_ref) * (1.0 / math.sqrt(NX * NY * NZ))
     own = all_modes[pl.ds(pl.multiple_of(16 * grp, 16), 16), :]
-    own_modes[...] = own
     shifted = jnp.concatenate([own * scale_all[s, 0:1, :] for s in range(N_GRP)], 0)
+    shifted_modes[...] = shifted
     row_mode = lax.broadcasted_iota(jnp.int32, (64, 128), 0) % 16
     spread = jnp.concatenate(
         [jnp.where(row_mode == k, shifted, 0.0).astype(BF16) for k in range(16)], 1
@@ -460,7 +507,7 @@
     )
     send_all(back, landed, send_sems.at[3], recv_sems.at[3], me)
     lax.fori_loop(5, 8, local_some, 0)
-    for copy in copies[7:]:
+    for copy in copies[7:10]:
         copy.wait()
     for part in range(8):
         wait_field(cotan, cotan_in, cotan_sems, part)
@@ -468,21 +515,21 @@
 
     fill_along_z(landed, ez_ref, along_z)
 
-    def some_cells(part, carry):
-        for pair in range(2):
-            cells_step(
-                2 * part + pair, along_z, local, bias_ref, cotan_in, ey_ref, ty_ref, out_held,
-                cotan_rows, bias_sum, along_y,
+    slots = ((pre_even, cotan_even), (pre_odd, cotan_odd))
+    for step in range(10):
+        if step < 8:
+            synthesis(step, along_z, local, ey_ref, slots[step % 2][0])
+        if 0 < step < 9:
+            pre_act, cotan_pre = slots[(step - 1) % 2]
+            activation(step - 1, pre_act, cotan_in, out_held, cotan_pre)
+            rows = pl.ds(8 * (step - 1), 8)
+            pltpu.make_async_copy(
+                out_held.at[rows], out_hbm.at[rows], out_sems.at[step - 1]
+            ).start()
+        if step > 1:
+            gradient_modes(
+                step - 2, slots[step % 2][1], ty_ref, cotan_rows, bias_sum, along_y
             )
-        return carry
-
-    def cells_part(part, carry):
-        lax.fori_loop(2 * part, 2 * part + 2, some_cells, 0)
-        rows = pl.ds(8 * part, 8)
-        pltpu.make_async_copy(out_held.at[rows], out_hbm.at[rows], out_sems.at[part]).start()
-        return carry
-
-    lax.fori_loop(0, 8, cells_part, 0)
 
     grad = jnp.zeros((512, 512), F32)
     for part in range(8):
@@ -547,15 +594,18 @@
 
     lax.fori_loop(1, N_LOW, collect, 0)
     wait_blocks(mixed_g, gathered_g, send_sems.at[7], recv_sems.at[7], N_GRP - 1, me)
-    modes_out[...] = gathered_g[...]
+    weight_terms(gathered_g, shifted_modes, d_spec)
+    spec_copy = pltpu.make_async_copy(d_spec, spec_hbm, out_sems.at[8])
+    spec_copy.start()
     for part in range(8):
         rows = pl.ds(8 * part, 8)
         pltpu.make_async_copy(out_held.at[rows], out_hbm.at[rows], out_sems.at[part]).wait()
     wait_blocks(third, third, send_sems.at[8], recv_sems.at[8], N_LOW - 1, me)
     sums_out[...] = third[...]
-
-
-def layer_call(field, cotangent, w_spec, w_local, scale_rows, bias):
+    spec_copy.wait()
+
+
+def layer_call(field, cotangent, w_spec, w_local, direction, shift, bias):
     vmem = pl.BlockSpec(memory_space=pltpu.VMEM)
     hbm = pl.BlockSpec(memory_space=pl.ANY)
     tables = (
@@ -569,17 +619,17 @@
         layer_kernel,
         out_shape=(
             jax.ShapeDtypeStruct(cells, BF16),
-            jax.ShapeDtypeStruct((4, 16, 128), BF16),
-            jax.ShapeDtypeStruct((16, 128), F32),
-            jax.ShapeDtypeStruct((4, 8, 128), F32),
+            jax.ShapeDtypeStruct((16, 64, 128), F32),
             jax.ShapeDtypeStruct((8, 8, 128), F32),
         ),
-        in_specs=[hbm] * 5 + [pl.BlockSpec(memory_space=pltpu.SMEM)] + [hbm] * 7,
-        out_specs=(hbm,) + (vmem,) * 4,
+        in_specs=[hbm] * 6 + [pl.BlockSpec(memory_space=pltpu.SMEM)] + [hbm] * 7,
+        out_specs=(hbm, hbm, vmem),
         scratch_shapes=[pltpu.VMEM(table.shape, BF16) for table in tables]
         + [
             pltpu.VMEM((16, 64, 128), BF16),
             pltpu.VMEM((64, 64), BF16),
+            pltpu.VMEM((64, BITS), jnp.int32),
+            pltpu.VMEM((1, 64), jnp.int32),
             pltpu.VMEM((8, 128), F32),
             pltpu.VMEM(cells, BF16),
             pltpu.VMEM(cells, BF16),
@@ -591,11 +641,18 @@
             pltpu.VMEM((4096, 128), F32),
             pltpu.VMEM((512, 512), BF16),
             pltpu.VMEM((2048, 128), BF16),
+            pltpu.VMEM((16, 64, 128), F32),
+            pltpu.VMEM((256, 1024), BF16),
+            pltpu.VMEM((256, 1024), BF16),
+            pltpu.VMEM((256, 1024), BF16),
+            pltpu.VMEM((256, 1024), BF16),
+            pltpu.VMEM((64, 8, 128), F32),
             blocks, blocks, quads, quads, blocks, blocks, blocks, blocks, quads, quads,
+            pltpu.VMEM((64, 128), F32),
             pltpu.VMEM((64, 128), F32),
             pltpu.VMEM((4, 8, 128), F32),
             pltpu.VMEM((4, 8, 128), F32),
-            pltpu.VMEM((64, 8, 128), F32),
+            pltpu.VMEM((64, 16, 128), F32),
             pltpu.VMEM((8, 8, 128), F32),
             pltpu.VMEM((8, 8, 128), F32),
             pltpu.VMEM((32, 8, 128), F32),
@@ -603,56 +660,45 @@
             pltpu.VMEM((8, 8, 128), F32),
             pltpu.SemaphoreType.DMA((8,)),
             pltpu.SemaphoreType.DMA((8,)),
-            pltpu.SemaphoreType.DMA((10,)),
-            pltpu.SemaphoreType.DMA((8,)),
+            pltpu.SemaphoreType.DMA((11,)),
+            pltpu.SemaphoreType.DMA((9,)),
             pltpu.SemaphoreType.DMA((9,)),
             pltpu.SemaphoreType.DMA((9,)),
         ],
         compiler_params=pltpu.CompilerParams(
             collective_id=0, has_side_effects=True, vmem_limit_bytes=58 * MIB
         ),
-    )(field, cotangent, w_spec, w_local, scale_rows, bias, *tables)
-
-
-def weights_kernel(
-    out_hbm, modes_hbm, own_hbm, scales_hbm, sums_hbm,
-    output, d_spec, d_local, d_bias,
-    held, modes_g, own_modes, scales, sums_ref, sems, in_sems, out_sems,
+    )(field, cotangent, w_spec, w_local, direction, shift, bias, *tables)
+
+
+def results_kernel(
+    out_hbm, spec_hbm, sums_hbm,
+    output, spec_out, d_local, d_bias,
+    held, spec_held, sums_ref, in_sems, out_sems,
 ):
-    small = [
-        (modes_hbm, modes_g), (own_hbm, own_modes), (scales_hbm, scales), (sums_hbm, sums_ref)
-    ]
-    copies = [
-        pltpu.make_async_copy(source, target, sems.at[at])
-        for at, (source, target) in enumerate(small)
-    ]
-    for copy in copies:
-        copy.start()
-    ins = []
-    outs = []
+    moves = []
     for part in range(8):
         rows = pl.ds(8 * part, 8)
-        ins.append(pltpu.make_async_copy(out_hbm.at[rows], held.at[rows], in_sems.at[part]))
-        outs.append(pltpu.make_async_copy(held.at[rows], output.at[rows], out_sems.at[part]))
+        moves.append((out_hbm.at[rows], held.at[rows], output.at[rows]))
+    for part in range(2):
+        rows = pl.ds(8 * part, 8)
+        moves.append((spec_hbm.at[rows], spec_held.at[rows], spec_out.at[rows]))
+    ins = [
+        pltpu.make_async_copy(source, middle, in_sems.at[at])
+        for at, (source, middle, _) in enumerate(moves)
+    ]
+    outs = [
+        pltpu.make_async_copy(middle, target, out_sems.at[at])
+        for at, (_, middle, target) in enumerate(moves)
+    ]
+    sums_copy = pltpu.make_async_copy(sums_hbm, sums_ref, in_sems.at[10])
     for copy in ins:
         copy.start()
-    for copy in copies:
-        copy.wait()
-    own = own_modes[...]
-    shifted = jnp.concatenate([own * scales[s, 0:1, :] for s in range(N_GRP)], 0)
-    columns = shifted.T
-    rows = modes_g[...].astype(F32).reshape(64, 128)
-    other = turned(rows, 1.0, -1.0)
-    for k in range(16):
-        total = jnp.zeros((64, 128), F32)
-        for s in range(N_GRP):
-            at = s * 16 + k
-            total = total + columns[0:64, at : at + 1] * rows[at : at + 1]
-            total = total + columns[64:128, at : at + 1] * other[at : at + 1]
-        d_spec[k] = total
-        if k % 2:
-            ins[k // 2].wait()
-            outs[k // 2].start()
+    sums_copy.start()
+    for before, after in zip(ins, outs):
+        before.wait()
+        after.start()
+    sums_copy.wait()
     sums = sums_ref[...].reshape(64, 128)
     d_local[...] = sums[:, 0:64]
     d_bias[...] = sums[0:1, 64:128]
@@ -660,48 +706,35 @@
         copy.wait()
 
 
-def weights_call(out, modes_g, own_modes, scales, sums):
+def results_call(out, d_spec, sums):
     vmem = pl.BlockSpec(memory_space=pltpu.VMEM)
     hbm = pl.BlockSpec(memory_space=pl.ANY)
     return pl.pallas_call(
-        weights_kernel,
+        results_kernel,
         out_shape=(
             jax.ShapeDtypeStruct(out.shape, BF16),
-            jax.ShapeDtypeStruct((16, 64, 128), F32),
+            jax.ShapeDtypeStruct(d_spec.shape, F32),
             jax.ShapeDtypeStruct((64, 64), F32),
             jax.ShapeDtypeStruct((1, 64), F32),
         ),
-        in_specs=[hbm] * 5,
-        out_specs=(hbm,) + (vmem,) * 3,
+        in_specs=[hbm] * 3,
+        out_specs=(hbm, hbm, vmem, vmem),
         scratch_shapes=[
             pltpu.VMEM(out.shape, BF16),
-            pltpu.VMEM((4, 16, 128), BF16),
-            pltpu.VMEM((16, 128), F32),
-            pltpu.VMEM((4, 8, 128), F32),
+            pltpu.VMEM(d_spec.shape, F32),
             pltpu.VMEM((8, 8, 128), F32),
-            pltpu.SemaphoreType.DMA((4,)),
-            pltpu.SemaphoreType.DMA((8,)),
-            pltpu.SemaphoreType.DMA((8,)),
+            pltpu.SemaphoreType.DMA((11,)),
+            pltpu.SemaphoreType.DMA((10,)),
         ],
         compiler_params=pltpu.CompilerParams(vmem_limit_bytes=58 * MIB),
-    )(out, modes_g, own_modes, scales, sums)
+    )(out, d_spec, sums)
 
 
 def shards(base_field, cotangent, w_spec, w_local, bias, direction, shift):
-    number = lax.axis_index("grp") + 1
-    gray_code = jnp.bitwise_xor(number, number >> 1)
-    picked = [
-        jnp.where(gray_code >> bit_pos & 1 == 1, direction[:, bit_pos], 0)
-        for bit_pos in range(N_GRP.bit_length())
-    ]
-    mixed_bits = reduce(jnp.bitwise_xor, picked)
-    sobol_point = jnp.bitwise_xor(mixed_bits, shift[0]).astype(F32) * 2.0 ** (-30)
-    scale = 0.5 + sobol_point
-    scale_rows = jnp.broadcast_to(jnp.concatenate([scale, scale])[None, :], (8, 128))
-    out, modes_g, own_modes, scales, sums = layer_call(
-        base_field, cotangent[0], w_spec.reshape(16, 64, 128), w_local, scale_rows, bias
-    )
-    output, d_spec, d_local, d_bias = weights_call(out, modes_g, own_modes, scales, sums)
+    out, d_spec, sums = layer_call(
+        base_field, cotangent[0], w_spec.reshape(16, 64, 128), w_local, direction, shift, bias
+    )
+    output, d_spec, d_local, d_bias = results_call(out, d_spec, sums)
     return (output[None], d_spec.reshape(4, 4, 64, 128), d_local, d_bias.reshape(64))
 
 

time: 70.6 us -> 66.1 us (0.936)
  Pallas kernels: 68.4 us -> 63.7 us
  other arithmetic: 0.89 us -> 0 us
  local copies, waits for them, and re-layouts: 0.6 us -> 1.42 us
    pallas_call x1, Pallas kernels: 62.9 us -> 59 us  [layer_call(): pl.pallas_call(layer_kernel, out_shape=(jax.ShapeDtypeStruct(cells, BF16)...]
    unnamed x0 -> x1, local copies, waits for them, and re-layouts: none -> 1.42 us
    pallas_call x1, Pallas kernels: 5.51 us -> 4.69 us  [results_call(): pl.pallas_call(results_kernel, out_shape=(jax.ShapeDtypeStruct(out.shape,...]
    add x1 -> x0, other arithmetic: 0.81 us -> none  [shards(): scale = 0.5 + sobol_point]
where the time goes in v4:
time: 66.1 us; the launch traced here: 65.9 us
  Pallas kernels  63.7 us (96%)
  local copies, waits for them, and re-layouts  1.42 us (2%)
  between operations  0.82 us (1%)
    pallas_call x1, Pallas kernels, layer_call(): pl.pallas_call(layer_kernel, out_shape=(jax.ShapeDtypeStruct(cells, BF16)...  59 us
    pallas_call x1, Pallas kernels, results_call(): pl.pallas_call(results_kernel, out_shape=(jax.ShapeDtypeStruct(out.shape,...  4.69 us
    unnamed x1, local copies, waits for them, and re-layouts  1.42 us

profile of v4, /device:TPU:1, one launch (start us, length us, event | category | flops | bytes accessed | tf_op | source)
XLA Modules:
  0.0 65.9 jit_solution(15581431490569200708)
XLA Ops:
  0.6 1.4 %copy.18.direction_hbm = s32[64,30]{1,0:T(8,128)} copy(s32[64,30]{0,1:T(8,128)} %param.19) | data formatting | bytes 15360 | tf_op args[5]
  2.0 59.0 %shard_map.165 = (bf16[64,2,128,128]{3,2,1,0:T(8,128)(2,1)}, f32[16,64,128]{2,1,0:T(8,128)}, f32[8,8,128]{2,1,0:T(8,128)}) custom-call(bf16[64,2,128,128]{3,2,1,0:T(8,128)(2,1)} %field.1, bf16[64,2,128,128]{3,2,1,0:T(8,128)(2,1)} %bitcast.5, bf16[16,64,128]{2,1,0:T(8,128)(2,1)} %bitcast.6, bf16[64,64]{1,0:T(8,128)(2,1)} %wl_hbm.1, ...), custom_call_target="tpu_custom_call" | custom-call | tf_op jit(solution)/shard_map/pallas_call | solution.py:618
  61.0 4.7 %shard_map.166 = (bf16[64,2,128,128]{3,2,1,0:T(8,128)(2,1)}, f32[16,64,128]{2,1,0:T(8,128)}, f32[64,64]{1,0:T(8,128)}, f32[1,64]{1,0:T(1,128)}) custom-call(bf16[64,2,128,128]{3,2,1,0:T(8,128)(2,1)} %get-tuple-element.11.out_hbm, f32[16,64,128]{2,1,0:T(8,128)} %get-tuple-element.12.spec_hbm, f32[8,8,128]{2,1,0:T(8,128)} %get-tuple-element.13.sums_hbm), custom_call_target="tpu_custom_call" | custom-call | tf_op jit(solution)/shard_map/pallas_call | solution.py:712

commit v5 on v4

--- a/solution.py
+++ b/solution.py
@@ -138,23 +138,39 @@
                 ]
 
 
-def along_z_modes(along_y, zt_ref, slab_modes):
-    for quarter in range(4):
+def along_z_half(half, along_y, zt_ref, modes_z):
+    for part in range(2):
         rows = jnp.concatenate(
             [
-                along_y[part * 1024 + quarter * 256 : part * 1024 + quarter * 256 + 256, :]
-                for part in range(4)
+                jnp.concatenate(
+                    [
+                        along_y[
+                            cs_x * 1024 + jy * 64 + half * 32 : cs_x * 1024 + jy * 64 + half * 32 + 32,
+                            :,
+                        ]
+                        for jy in range(part * 8, part * 8 + 8)
+                    ],
+                    0,
+                ).astype(BF16)
+                for cs_x in range(4)
             ],
             1,
-        ).astype(BF16)
-        got = nt_dot(zt_ref[...], rows)
-        for jy in range(4):
-            real = got[0:32, jy * 64 : jy * 64 + 64]
-            imag = got[32:64, jy * 64 : jy * 64 + 64]
-            owner = (quarter * 4 + jy) * 4
-            slab_modes[owner : owner + 4] = (
-                jnp.concatenate([real, imag], 1).reshape(4, 8, 128).astype(BF16)
-            )
+        )
+        modes_z[half, part] = nt_dot(zt_ref[...], rows)
+
+
+def join_halves(modes_z, slab_modes):
+    for jy in range(16):
+        lanes = slice((jy % 8) * 32, (jy % 8) * 32 + 32)
+        block = jnp.concatenate(
+            [
+                modes_z[half, jy // 8, re * 32 : re * 32 + 32, lanes]
+                for re in range(2)
+                for half in range(2)
+            ],
+            1,
+        )
+        slab_modes[jy * 4 : jy * 4 + 4] = block.reshape(4, 8, 128).astype(BF16)
 
 
 def greet(barrier, me, grp):
@@ -240,14 +256,10 @@
 def scale_rows(grp, direction_ref, shift_ref):
     number = grp + 1
     gray_code = number ^ (number >> 1)
-    bits = jnp.zeros((64, 1), jnp.int32)
+    bits = shift_ref[...]
     for bit_pos in range(N_GRP.bit_length()):
-        bits = bits ^ (direction_ref[:, bit_pos : bit_pos + 1] * ((gray_code >> bit_pos) & 1))
-    diagonal = lax.broadcasted_iota(jnp.int32, (64, 64), 0) == lax.broadcasted_iota(
-        jnp.int32, (64, 64), 1
-    )
-    row = jnp.sum(jnp.where(diagonal, jnp.broadcast_to(bits, (64, 64)), 0), axis=0, keepdims=True)
-    scale = 0.5 + (row ^ shift_ref[...]).astype(F32) * 2.0 ** (-BITS)
+        bits = bits ^ (direction_ref[bit_pos : bit_pos + 1, :] * ((gray_code >> bit_pos) & 1))
+    scale = 0.5 + bits.astype(F32) * 2.0 ** (-BITS)
     return jnp.broadcast_to(jnp.concatenate([scale, scale], 1), (8, 128))
 
 
@@ -353,22 +365,23 @@
                 ] = block.astype(BF16)
 
 
-def sums_of(grad, bias_sum, scale_row):
+def local_grad(grad):
     same = (
-        lax.broadcasted_iota(jnp.int32, (512, 512), 0) % 8
-        == lax.broadcasted_iota(jnp.int32, (512, 512), 1) % 8
-    )
-    per_c = jnp.sum(jnp.where(same, grad, 0.0).reshape(64, 8, 512), axis=1)
+        lax.broadcasted_iota(jnp.int32, (256, 512), 0) % 8
+        == lax.broadcasted_iota(jnp.int32, (256, 512), 1) % 8
+    )
+    kept = jnp.where(same, grad, 0.0)
+    high = kept.astype(BF16)
+    low = (kept - high.astype(F32)).astype(BF16)
     pick = (
         lax.broadcasted_iota(jnp.int32, (512, 64), 0) // 8
         == lax.broadcasted_iota(jnp.int32, (512, 64), 1)
-    ).astype(F32)
-    d_local = jnp.dot(per_c, pick, preferred_element_type=F32, precision=lax.Precision.HIGHEST)
-    d_local = d_local * (scale_row[0:1, 0:64] * GRAD_SCALE)
-    lanes = jnp.sum(bias_sum[...], axis=1)
-    d_bias = nt_dot(jnp.full((8, 128), GRAD_SCALE, F32), lanes, lax.Precision.HIGHEST)
-    side = jnp.concatenate([d_bias, jnp.zeros((56, 64), F32)], 0)
-    return jnp.concatenate([d_local, side], 1).reshape(8, 8, 128)
+    )
+    pick = pick.astype(F32).astype(BF16)
+    got = jnp.dot(high, pick, preferred_element_type=F32) + jnp.dot(
+        low, pick, preferred_element_type=F32
+    )
+    return jnp.sum(got.reshape(32, 8, 64), axis=1)
 
 
 def weight_terms(gathered_g, shifted_modes, d_spec):
@@ -390,7 +403,7 @@
     out_hbm, spec_hbm, sums_out,
     ty_ref, ztf_ref, ztb_ref, tx_ref, txb_ref, ey_ref, ez_ref, w_ref, wl_ref, direction_ref, shift_ref, scale_ref,
     held, cotan_in, out_held, field_rows, cotan_rows, local, along_y, along_z, kron, w_two,
-    d_spec, pre_even, pre_odd, cotan_even, cotan_odd, bias_rows,
+    d_spec, modes_z, grad, pre_even, pre_odd, cotan_even, cotan_odd, bias_rows,
     slab_modes, pencil, mixed, gathered, back, landed, slab_g, pencil_g, mixed_g, gathered_g,
     all_modes, shifted_modes, scale_own, scale_all, bias_sum, own_sums, first, second, second_own, third,
     field_sems, cotan_sems, table_sems, out_sems, send_sems, recv_sems,
@@ -447,8 +460,11 @@
         got = jnp.dot(ty_ref[...], rows, preferred_element_type=F32)
         for pair in range(4):
             store_along_y(along_y, got[:, pair * 256 : pair * 256 + 256], 8 * part + 2 * pair)
-    copies[1].wait()
-    along_z_modes(along_y, ztf_ref, slab_modes)
+        if part == 3:
+            copies[1].wait()
+            along_z_half(0, along_y, ztf_ref, modes_z)
+    along_z_half(1, along_y, ztf_ref, modes_z)
+    join_halves(modes_z, slab_modes)
     copies[2].wait()
     copies[10].wait()
     scale_ref[...] = scale_rows(grp, direction_ref, shift_ref)
@@ -530,11 +546,23 @@
             gradient_modes(
                 step - 2, slots[step % 2][1], ty_ref, cotan_rows, bias_sum, along_y
             )
-
-    grad = jnp.zeros((512, 512), F32)
+        if step == 5:
+            along_z_half(0, along_y, ztb_ref, modes_z)
+            grad[...] = jnp.zeros_like(grad)
+        if step > 5:
+            for part in (2 * step - 12, 2 * step - 11):
+                grad[...] += nt_dot(cotan_rows[part, 0:256, :], field_rows[part])
+
+    d_top = local_grad(grad[...])
+    bottom = jnp.zeros((256, 512), F32)
     for part in range(8):
-        grad = grad + nt_dot(cotan_rows[part], field_rows[part])
-    own_sums[...] = sums_of(grad, bias_sum, scale_ref[...])
+        bottom = bottom + nt_dot(cotan_rows[part, 256:512, :], field_rows[part])
+    d_local = jnp.concatenate([d_top, local_grad(bottom)], 0)
+    d_local = d_local * (scale_ref[0:1, 0:64] * GRAD_SCALE)
+    lanes = jnp.sum(bias_sum[...], axis=1)
+    d_bias = nt_dot(jnp.full((8, 128), GRAD_SCALE, F32), lanes, lax.Precision.HIGHEST)
+    side = jnp.concatenate([d_bias, jnp.zeros((56, 64), F32)], 0)
+    own_sums[...] = jnp.concatenate([d_local, side], 1).reshape(8, 8, 128)
 
     def scatter(step, carry):
         other = lax.rem(low + step, N_LOW)
@@ -550,7 +578,8 @@
 
     lax.fori_loop(1, N_LOW, scatter, 0)
     first[pl.ds(low, 1)] = own_sums[pl.ds(low, 1)]
-    along_z_modes(along_y, ztb_ref, slab_g)
+    along_z_half(1, along_y, ztb_ref, modes_z)
+    join_halves(modes_z, slab_g)
     send_all(slab_g, pencil_g, send_sems.at[5], recv_sems.at[5], me)
     wait_blocks(own_sums, first, send_sems.at[4], recv_sems.at[4], N_LOW - 1, me)
     part_sum = jnp.sum(first[...], axis=0, keepdims=True)
@@ -628,7 +657,7 @@
         + [
             pltpu.VMEM((16, 64, 128), BF16),
             pltpu.VMEM((64, 64), BF16),
-            pltpu.VMEM((64, BITS), jnp.int32),
+            pltpu.VMEM((BITS, 64), jnp.int32),
             pltpu.VMEM((1, 64), jnp.int32),
             pltpu.VMEM((8, 128), F32),
             pltpu.VMEM(cells, BF16),
@@ -642,6 +671,8 @@
             pltpu.VMEM((512, 512), BF16),
             pltpu.VMEM((2048, 128), BF16),
             pltpu.VMEM((16, 64, 128), F32),
+            pltpu.VMEM((2, 2, 64, 256), F32),
+            pltpu.VMEM((256, 512), F32),
             pltpu.VMEM((256, 1024), BF16),
             pltpu.VMEM((256, 1024), BF16),
             pltpu.VMEM((256, 1024), BF16),
@@ -732,7 +763,7 @@
 
 def shards(base_field, cotangent, w_spec, w_local, bias, direction, shift):
     out, d_spec, sums = layer_call(
-        base_field, cotangent[0], w_spec.reshape(16, 64, 128), w_local, direction, shift, bias
+        base_field, cotangent[0], w_spec.reshape(16, 64, 128), w_local, direction.T, shift, bias
     )
     output, d_spec, d_local, d_bias = results_call(out, d_spec, sums)
     return (output[None], d_spec.reshape(4, 4, 64, 128), d_local, d_bias.reshape(64))

time: 66.1 us -> 65 us (0.983)
  local copies, waits for them, and re-layouts: 1.42 us -> 0 us
    unnamed x1 -> x0, local copies, waits for them, and re-layouts: 1.42 us -> none
where the time goes in v5:
time: 65 us; the launch traced here: 64.9 us
  Pallas kernels  64.1 us (99%)
  between operations  0.82 us (1%)
    pallas_call x1, Pallas kernels, layer_call(): pl.pallas_call(layer_kernel, out_shape=(jax.ShapeDtypeStruct(cells, BF16)...  59.4 us
    pallas_call x1, Pallas kernels, results_call(): pl.pallas_call(results_kernel, out_shape=(jax.ShapeDtypeStruct(out.shape,...  4.69 us

profile of v5, /device:TPU:1, one launch (start us, length us, event | category | flops | bytes accessed | tf_op | source)
XLA Modules:
  0.0 64.9 jit_solution(15067041383639167720)
XLA Ops:
  0.6 59.4 %shard_map.165 = (bf16[64,2,128,128]{3,2,1,0:T(8,128)(2,1)}, f32[16,64,128]{2,1,0:T(8,128)}, f32[8,8,128]{2,1,0:T(8,128)}) custom-call(bf16[64,2,128,128]{3,2,1,0:T(8,128)(2,1)} %field.1, bf16[64,2,128,128]{3,2,1,0:T(8,128)(2,1)} %bitcast.6, bf16[16,64,128]{2,1,0:T(8,128)(2,1)} %bitcast.7, bf16[64,64]{1,0:T(8,128)(2,1)} %wl_hbm.1, s32[30,64]{1,0:T(8,128)} %bitcast.8, ...), custom_call_target="tpu_custom_call" | custom-call | tf_op jit(solution)/shard_map/pallas_call | solution.py:647
  60.1 4.7 %shard_map.166 = (bf16[64,2,128,128]{3,2,1,0:T(8,128)(2,1)}, f32[16,64,128]{2,1,0:T(8,128)}, f32[64,64]{1,0:T(8,128)}, f32[1,64]{1,0:T(1,128)}) custom-call(bf16[64,2,128,128]{3,2,1,0:T(8,128)(2,1)} %get-tuple-element.11.out_hbm, f32[16,64,128]{2,1,0:T(8,128)} %get-tuple-element.12.spec_hbm, f32[8,8,128]{2,1,0:T(8,128)} %get-tuple-element.13.sums_hbm), custom_call_target="tpu_custom_call" | custom-call | tf_op jit(solution)/shard_map/pallas_call | solution.py:743

commit v6 on v5

--- a/solution.py
+++ b/solution.py
@@ -1,3 +1,4 @@
+import functools
 import math
 
 import jax
@@ -173,18 +174,25 @@
         slab_modes[jy * 4 : jy * 4 + 4] = block.reshape(4, 8, 128).astype(BF16)
 
 
-def greet(barrier, me, grp):
-    def tell(step, carry):
-        pl.semaphore_signal(
-            barrier, inc=1, device_id={"slab": lax.rem(me + step, N_SLAB)}, device_id_type=MESH
-        )
-        return carry
-
-    lax.fori_loop(1, N_SLAB, tell, 0)
-    for step in range(1, N_GRP):
-        pl.semaphore_signal(
-            barrier, inc=1, device_id={"grp": lax.rem(grp + step, N_GRP)}, device_id_type=MESH
-        )
+def greetings(barrier, me, grp, low, z):
+    def tell(device):
+        pl.semaphore_signal(barrier, inc=1, device_id=device, device_id_type=MESH)
+
+    calls = []
+    for dz in (4, 3, 5, 2, 6, 1, 7, 0):
+        other_z = lax.rem(z + dz, N_Z) * N_LOW
+        for g_step in (2, 1, 3):
+            calls.append(
+                functools.partial(
+                    tell, {"grp": lax.rem(grp + g_step, N_GRP), "slab": other_z + low}
+                )
+            )
+        for step in (4, 5, 2, 3, 6, 7, 1, 0):
+            if dz or step:
+                calls.append(
+                    functools.partial(tell, {"slab": other_z + lax.rem(low + step, N_LOW)})
+                )
+    return calls
 
 
 def send_all(source, target, send_sem, recv_sem, me):
@@ -384,17 +392,19 @@
     return jnp.sum(got.reshape(32, 8, 64), axis=1)
 
 
-def weight_terms(gathered_g, shifted_modes, d_spec):
-    columns = shifted_modes[...].T
-    rows = gathered_g[...].astype(F32).reshape(64, 128)
-    other = turned(rows, 1.0, -1.0)
+def fill_terms(shifted_modes, terms):
+    turn = shifted_modes[...].T
+    columns = jnp.concatenate([turn[0:64], turn[64:128]], 1)
+    mode = lax.broadcasted_iota(jnp.int32, (64, 128), 1) % 16
     for k in range(16):
-        total = jnp.zeros((64, 128), F32)
-        for s in range(N_GRP):
-            at = s * 16 + k
-            total = total + columns[0:64, at : at + 1] * rows[at : at + 1]
-            total = total + columns[64:128, at : at + 1] * other[at : at + 1]
-        d_spec[k] = total
+        terms[k * 64 : k * 64 + 64, :] = jnp.where(mode == k, columns, 0.0).astype(BF16)
+
+
+def weight_terms(gathered_g, terms, d_spec):
+    rows = gathered_g[...].reshape(64, 128)
+    both = jnp.concatenate([rows, turned(rows.astype(F32), 1.0, -1.0).astype(BF16)], 0)
+    got = jnp.dot(terms[...], both, preferred_element_type=F32)
+    d_spec[...] = got.reshape(16, 64, 128)
 
 
 def layer_kernel(
@@ -403,7 +413,7 @@
     out_hbm, spec_hbm, sums_out,
     ty_ref, ztf_ref, ztb_ref, tx_ref, txb_ref, ey_ref, ez_ref, w_ref, wl_ref, direction_ref, shift_ref, scale_ref,
     held, cotan_in, out_held, field_rows, cotan_rows, local, along_y, along_z, kron, w_two,
-    d_spec, modes_z, grad, pre_even, pre_odd, cotan_even, cotan_odd, bias_rows,
+    d_spec, terms, modes_z, grad, pre_even, pre_odd, cotan_even, cotan_odd, bias_rows,
     slab_modes, pencil, mixed, gathered, back, landed, slab_g, pencil_g, mixed_g, gathered_g,
     all_modes, shifted_modes, scale_own, scale_all, bias_sum, own_sums, first, second, second_own, third,
     field_sems, cotan_sems, table_sems, out_sems, send_sems, recv_sems,
@@ -428,26 +438,15 @@
     for copy in copies[2:]:
         copy.start()
     fetch_field(cotan, cotan_in, cotan_sems)
-    greet(barrier, me, grp)
-    for g_step in range(1, N_GRP):
-
-        def tell(step, carry):
-            pl.semaphore_signal(
-                barrier,
-                inc=1,
-                device_id={
-                    "grp": lax.rem(grp + g_step, N_GRP),
-                    "slab": lax.rem(z + step, N_Z) * N_LOW + low,
-                },
-                device_id_type=MESH,
-            )
-            return carry
-
-        lax.fori_loop(1, N_Z, tell, 0)
-
+    calls = greetings(barrier, me, grp, low, z)
+
+    for call in calls[:15]:
+        call()
     copies[0].wait()
 
     for part in range(8):
+        for call in calls[15 * part + 15 : 15 * part + 30]:
+            call()
         wait_field(field, held, field_sems, part)
         rows = jnp.concatenate(
             [
@@ -523,6 +522,7 @@
     )
     send_all(back, landed, send_sems.at[3], recv_sems.at[3], me)
     lax.fori_loop(5, 8, local_some, 0)
+    fill_terms(shifted_modes, terms)
     for copy in copies[7:10]:
         copy.wait()
     for part in range(8):
@@ -623,7 +623,7 @@
 
     lax.fori_loop(1, N_LOW, collect, 0)
     wait_blocks(mixed_g, gathered_g, send_sems.at[7], recv_sems.at[7], N_GRP - 1, me)
-    weight_terms(gathered_g, shifted_modes, d_spec)
+    weight_terms(gathered_g, terms, d_spec)
     spec_copy = pltpu.make_async_copy(d_spec, spec_hbm, out_sems.at[8])
     spec_copy.start()
     for part in range(8):
@@ -671,6 +671,7 @@
             pltpu.VMEM((512, 512), BF16),
             pltpu.VMEM((2048, 128), BF16),
             pltpu.VMEM((16, 64, 128), F32),
+            pltpu.VMEM((1024, 128), BF16),
             pltpu.VMEM((2, 2, 64, 256), F32),
             pltpu.VMEM((256, 512), F32),
             pltpu.VMEM((256, 1024), BF16),

time: 65 us -> 65.6 us (level)
  no operation moved by 1% of the time
where the time goes in v6:
time: 65.6 us; the launch traced here: 65.5 us
  Pallas kernels  64.7 us (99%)
  between operations  0.8 us (1%)
    pallas_call x1, Pallas kernels, layer_call(): pl.pallas_call(layer_kernel, out_shape=(jax.ShapeDtypeStruct(cells, BF16)...  60 us
    pallas_call x1, Pallas kernels, results_call(): pl.pallas_call(results_kernel, out_shape=(jax.ShapeDtypeStruct(out.shape,...  4.69 us

profile of v6, /device:TPU:1, one launch (start us, length us, event | category | flops | bytes accessed | tf_op | source)
XLA Modules:
  0.0 65.5 jit_solution(11335684569436544195)
XLA Ops:
  0.6 60.0 %shard_map.165 = (bf16[64,2,128,128]{3,2,1,0:T(8,128)(2,1)}, f32[16,64,128]{2,1,0:T(8,128)}, f32[8,8,128]{2,1,0:T(8,128)}) custom-call(bf16[64,2,128,128]{3,2,1,0:T(8,128)(2,1)} %field.1, bf16[64,2,128,128]{3,2,1,0:T(8,128)(2,1)} %bitcast.6, bf16[16,64,128]{2,1,0:T(8,128)(2,1)} %bitcast.7, bf16[64,64]{1,0:T(8,128)(2,1)} %wl_hbm.1, s32[30,64]{1,0:T(8,128)} %bitcast.8, ...), custom_call_target="tpu_custom_call" | custom-call | tf_op jit(solution)/shard_map/pallas_call | solution.py:647
  60.6 4.7 %shard_map.166 = (bf16[64,2,128,128]{3,2,1,0:T(8,128)(2,1)}, f32[16,64,128]{2,1,0:T(8,128)}, f32[64,64]{1,0:T(8,128)}, f32[1,64]{1,0:T(1,128)}) custom-call(bf16[64,2,128,128]{3,2,1,0:T(8,128)(2,1)} %get-tuple-element.11.out_hbm, f32[16,64,128]{2,1,0:T(8,128)} %get-tuple-element.12.spec_hbm, f32[8,8,128]{2,1,0:T(8,128)} %get-tuple-element.13.sums_hbm), custom_call_target="tpu_custom_call" | custom-call | tf_op jit(solution)/shard_map/pallas_call | solution.py:744

commit v7 on v6

--- a/solution.py
+++ b/solution.py
@@ -26,7 +26,7 @@
 MIB = 1024 * 1024
 GELU_K = math.sqrt(2.0 / math.pi)
 GELU_A = 0.044715
-GRAD_SCALE = 1.0 / math.sqrt(N_GRP * NX * NY * NZ)
+GRAD_SCALE = 0.5 / math.sqrt(N_GRP * NX * NY * NZ)
 
 
 def waves(length, half):
@@ -344,15 +344,15 @@
                 square = pre * pre
                 inner = pre * (1.0 + GELU_A * square)
                 tanh = jnp.tanh(inner.astype(F32) * GELU_K)
-                half = 0.5 + 0.5 * tanh
-                bell = (half * (GELU_K - GELU_K * tanh)).astype(BF16)
-                half = half.astype(BF16)
-                out_held[channel, x] = pre * half
-                slope = half + bell * (pre * (1.0 + (3.0 * GELU_A) * square))
+                above = 1.0 + tanh
+                bell = (above * (1.0 - tanh)).astype(BF16)
+                above = above.astype(BF16)
+                out_held[channel, x] = (0.5 * pre) * above
+                slope = above + bell * (pre * (GELU_K + (3.0 * GELU_K * GELU_A) * square))
                 cotan_pre[at, lanes] = slope * cotan_in[channel, x]
 
 
-def gradient_modes(group, cotan_pre, ty_ref, cotan_rows, bias_sum, along_y):
+def gradient_modes(group, cotan_pre, ty_ref, cotan_rows, along_y):
     got = jnp.dot(ty_ref[...], cotan_pre[...], preferred_element_type=F32)
     for pair in range(4):
         store_along_y(along_y, got[:, pair * 256 : pair * 256 + 256], 8 * group + 2 * pair)
@@ -360,9 +360,6 @@
         for x in range(2):
             lanes = slice(pair * 256 + x * 128, pair * 256 + x * 128 + 128)
             wide = cotan_pre[:, lanes].astype(F32)
-            sums = jnp.sum(wide.reshape(2, 16, 8, 128), axis=1)
-            for c2 in range(2):
-                bias_sum[8 * group + 2 * pair + c2, x * 8 : x * 8 + 8] = sums[c2]
             for y8 in range(16):
                 block = jnp.concatenate(
                     [wide[c2 * 128 + 8 * y8 : c2 * 128 + 8 * y8 + 8] for c2 in range(2)], 0
@@ -415,7 +412,7 @@
     held, cotan_in, out_held, field_rows, cotan_rows, local, along_y, along_z, kron, w_two,
     d_spec, terms, modes_z, grad, pre_even, pre_odd, cotan_even, cotan_odd, bias_rows,
     slab_modes, pencil, mixed, gathered, back, landed, slab_g, pencil_g, mixed_g, gathered_g,
-    all_modes, shifted_modes, scale_own, scale_all, bias_sum, own_sums, first, second, second_own, third,
+    all_modes, shifted_modes, scale_own, scale_all, own_sums, first, second, second_own, third,
     field_sems, cotan_sems, table_sems, out_sems, send_sems, recv_sems,
 ):
     me = lax.axis_index("slab")
@@ -437,7 +434,6 @@
     fetch_field(field, held, field_sems)
     for copy in copies[2:]:
         copy.start()
-    fetch_field(cotan, cotan_in, cotan_sems)
     calls = greetings(barrier, me, grp, low, z)
 
     for call in calls[:15]:
@@ -472,6 +468,7 @@
     pl.semaphore_wait(barrier, N_SLAB - 1 + N_GRP - 1 + (N_GRP - 1) * (N_Z - 1))
     send_all(slab_modes, pencil, send_sems.at[0], recv_sems.at[0], me)
     send_grp(scale_own, scale_all, send_sems.at[1], recv_sems.at[1], grp, False)
+    fetch_field(cotan, cotan_in, cotan_sems)
 
     copies[3].wait()
     copies[4].wait()
@@ -544,7 +541,7 @@
             ).start()
         if step > 1:
             gradient_modes(
-                step - 2, slots[step % 2][1], ty_ref, cotan_rows, bias_sum, along_y
+                step - 2, slots[step % 2][1], ty_ref, cotan_rows, along_y
             )
         if step == 5:
             along_z_half(0, along_y, ztb_ref, modes_z)
@@ -559,7 +556,7 @@
         bottom = bottom + nt_dot(cotan_rows[part, 256:512, :], field_rows[part])
     d_local = jnp.concatenate([d_top, local_grad(bottom)], 0)
     d_local = d_local * (scale_ref[0:1, 0:64] * GRAD_SCALE)
-    lanes = jnp.sum(bias_sum[...], axis=1)
+    lanes = along_y[0:64, :] + along_y[1024:1088, :]
     d_bias = nt_dot(jnp.full((8, 128), GRAD_SCALE, F32), lanes, lax.Precision.HIGHEST)
     side = jnp.concatenate([d_bias, jnp.zeros((56, 64), F32)], 0)
     own_sums[...] = jnp.concatenate([d_local, side], 1).reshape(8, 8, 128)
@@ -684,7 +681,6 @@
             pltpu.VMEM((64, 128), F32),
             pltpu.VMEM((4, 8, 128), F32),
             pltpu.VMEM((4, 8, 128), F32),
-            pltpu.VMEM((64, 16, 128), F32),
             pltpu.VMEM((8, 8, 128), F32),
             pltpu.VMEM((8, 8, 128), F32),
             pltpu.VMEM((32, 8, 128), F32),

time: 65.6 us -> 64.9 us (0.989)
  Pallas kernels: 64.7 us -> 64 us
where the time goes in v7:
time: 64.9 us
  Pallas kernels  64 us (99%)
  between operations  0.8 us (1%)
    pallas_call x1, Pallas kernels, layer_call(): pl.pallas_call(layer_kernel, out_shape=(jax.ShapeDtypeStruct(cells, BF16)...  59.4 us
    pallas_call x1, Pallas kernels, results_call(): pl.pallas_call(results_kernel, out_shape=(jax.ShapeDtypeStruct(out.shape,...  4.69 us

profile of v7, /device:TPU:1, one launch (start us, length us, event | category | flops | bytes accessed | tf_op | source)
XLA Modules:
  0.0 64.9 jit_solution(1393829482403700587)
XLA Ops:
  0.6 59.4 %shard_map.165 = (bf16[64,2,128,128]{3,2,1,0:T(8,128)(2,1)}, f32[16,64,128]{2,1,0:T(8,128)}, f32[8,8,128]{2,1,0:T(8,128)}) custom-call(bf16[64,2,128,128]{3,2,1,0:T(8,128)(2,1)} %field.1, bf16[64,2,128,128]{3,2,1,0:T(8,128)(2,1)} %bitcast.6, bf16[16,64,128]{2,1,0:T(8,128)(2,1)} %bitcast.7, bf16[64,64]{1,0:T(8,128)(2,1)} %wl_hbm.1, s32[30,64]{1,0:T(8,128)} %bitcast.8, ...), custom_call_target="tpu_custom_call" | custom-call | tf_op jit(solution)/shard_map/pallas_call | solution.py:644
  60.0 4.7 %shard_map.166 = (bf16[64,2,128,128]{3,2,1,0:T(8,128)(2,1)}, f32[16,64,128]{2,1,0:T(8,128)}, f32[64,64]{1,0:T(8,128)}, f32[1,64]{1,0:T(1,128)}) custom-call(bf16[64,2,128,128]{3,2,1,0:T(8,128)(2,1)} %get-tuple-element.11.out_hbm, f32[16,64,128]{2,1,0:T(8,128)} %get-tuple-element.12.spec_hbm, f32[8,8,128]{2,1,0:T(8,128)} %get-tuple-element.13.sums_hbm), custom_call_target="tpu_custom_call" | custom-call | tf_op jit(solution)/shard_map/pallas_call | solution.py:740

commit v8 on v7

--- a/solution.py
+++ b/solution.py
@@ -228,7 +228,7 @@
 
 
 def send_grp(source, target, send_sem, recv_sem, grp, by_target):
-    for step in range(1, N_GRP):
+    for step in (2, 1, 3):
         other = lax.rem(grp + step, N_GRP)
         pltpu.make_async_remote_copy(
             src_ref=source.at[other] if by_target else source.at[grp],
@@ -484,7 +484,7 @@
         local_step(part, held, kron, bias_rows, field_rows, local)
         return carry
 
-    lax.fori_loop(0, 3, local_some, 0)
+    lax.fori_loop(0, 1, local_some, 0)
     pltpu.make_async_remote_copy(
         src_ref=scale_own.at[pl.ds(0, N_GRP - 1)],
         dst_ref=scale_all.at[pl.ds(0, N_GRP - 1)],
@@ -510,7 +510,7 @@
     )
     send_grp(mixed, gathered, send_sems.at[2], recv_sems.at[2], grp, True)
     gathered[pl.ds(grp, 1)] = mixed[pl.ds(grp, 1)]
-    lax.fori_loop(3, 5, local_some, 0)
+    lax.fori_loop(1, 5, local_some, 0)
     wait_blocks(mixed, gathered, send_sems.at[2], recv_sems.at[2], N_GRP - 1, me)
     full = gathered[...].reshape(64, 128)
     both = jnp.concatenate([full, turned(full.astype(F32), -1.0, 1.0).astype(BF16)], 0)
@@ -605,12 +605,14 @@
     send_grp(mixed_g, gathered_g, send_sems.at[7], recv_sems.at[7], grp, True)
     gathered_g[pl.ds(grp, 1)] = mixed_g[pl.ds(grp, 1)]
     wait_blocks(second, second, send_sems.at[6], recv_sems.at[6], N_GRP * N_Z - 1, me)
-    third[pl.ds(low, 1)] = jnp.sum(second[...], axis=0, keepdims=True)
+    third[...] = jnp.sum(second[...], axis=0, keepdims=True)
+    own_copy = pltpu.make_async_copy(third.at[0], sums_out.at[low], out_sems.at[9])
+    own_copy.start()
 
     def collect(step, carry):
         pltpu.make_async_remote_copy(
-            src_ref=third.at[low],
-            dst_ref=third.at[low],
+            src_ref=third.at[0],
+            dst_ref=sums_out.at[low],
             send_sem=send_sems.at[8],
             recv_sem=recv_sems.at[8],
             device_id={"slab": z * N_LOW + lax.rem(low + step, N_LOW)},
@@ -626,13 +628,12 @@
     for part in range(8):
         rows = pl.ds(8 * part, 8)
         pltpu.make_async_copy(out_held.at[rows], out_hbm.at[rows], out_sems.at[part]).wait()
-    wait_blocks(third, third, send_sems.at[8], recv_sems.at[8], N_LOW - 1, me)
-    sums_out[...] = third[...]
+    wait_blocks(sums_out, sums_out, send_sems.at[8], recv_sems.at[8], N_LOW - 1, me)
+    own_copy.wait()
     spec_copy.wait()
 
 
 def layer_call(field, cotangent, w_spec, w_local, direction, shift, bias):
-    vmem = pl.BlockSpec(memory_space=pltpu.VMEM)
     hbm = pl.BlockSpec(memory_space=pl.ANY)
     tables = (
         table_ty(), table_zt(False), table_zt(True), table_tx(),
@@ -649,7 +650,7 @@
             jax.ShapeDtypeStruct((8, 8, 128), F32),
         ),
         in_specs=[hbm] * 6 + [pl.BlockSpec(memory_space=pltpu.SMEM)] + [hbm] * 7,
-        out_specs=(hbm, hbm, vmem),
+        out_specs=(hbm,) * 3,
         scratch_shapes=[pltpu.VMEM(table.shape, BF16) for table in tables]
         + [
             pltpu.VMEM((16, 64, 128), BF16),
@@ -685,11 +686,11 @@
             pltpu.VMEM((8, 8, 128), F32),
             pltpu.VMEM((32, 8, 128), F32),
             pltpu.VMEM((1, 8, 128), F32),
-            pltpu.VMEM((8, 8, 128), F32),
+            pltpu.VMEM((1, 8, 128), F32),
             pltpu.SemaphoreType.DMA((8,)),
             pltpu.SemaphoreType.DMA((8,)),
             pltpu.SemaphoreType.DMA((11,)),
-            pltpu.SemaphoreType.DMA((9,)),
+            pltpu.SemaphoreType.DMA((10,)),
             pltpu.SemaphoreType.DMA((9,)),
             pltpu.SemaphoreType.DMA((9,)),
         ],

time: 64.9 us -> 64.4 us (level)
  no operation moved by 1% of the time
where the time goes in v8:
time: 64.4 us; the launch traced here: 64.3 us
  Pallas kernels  63.5 us (99%)
  between operations  0.8 us (1%)
    pallas_call x1, Pallas kernels, layer_call(): pl.pallas_call(layer_kernel, out_shape=(jax.ShapeDtypeStruct(cells, BF16)...  58.8 us
    pallas_call x1, Pallas kernels, results_call(): pl.pallas_call(results_kernel, out_shape=(jax.ShapeDtypeStruct(out.shape,...  4.69 us

profile of v8, /device:TPU:1, one launch (start us, length us, event | category | flops | bytes accessed | tf_op | source)
XLA Modules:
  0.0 64.3 jit_solution(11180480887161100878)
XLA Ops:
  0.6 58.8 %shard_map.165 = (bf16[64,2,128,128]{3,2,1,0:T(8,128)(2,1)}, f32[16,64,128]{2,1,0:T(8,128)}, f32[8,8,128]{2,1,0:T(8,128)}) custom-call(bf16[64,2,128,128]{3,2,1,0:T(8,128)(2,1)} %field.1, bf16[64,2,128,128]{3,2,1,0:T(8,128)(2,1)} %bitcast.6, bf16[16,64,128]{2,1,0:T(8,128)(2,1)} %bitcast.7, bf16[64,64]{1,0:T(8,128)(2,1)} %wl_hbm.1, s32[30,64]{1,0:T(8,128)} %bitcast.8, ...), custom_call_target="tpu_custom_call" | custom-call | tf_op jit(solution)/shard_map/pallas_call | solution.py:645
  59.5 4.7 %shard_map.166 = (bf16[64,2,128,128]{3,2,1,0:T(8,128)(2,1)}, f32[16,64,128]{2,1,0:T(8,128)}, f32[64,64]{1,0:T(8,128)}, f32[1,64]{1,0:T(1,128)}) custom-call(bf16[64,2,128,128]{3,2,1,0:T(8,128)(2,1)} %get-tuple-element.11.out_hbm, f32[16,64,128]{2,1,0:T(8,128)} %get-tuple-element.12.spec_hbm, f32[8,8,128]{2,1,0:T(8,128)} %get-tuple-element.13.sums_hbm), custom_call_target="tpu_custom_call" | custom-call | tf_op jit(solution)/shard_map/pallas_call | solution.py:741

commit v9 on v8

--- a/solution.py
+++ b/solution.py
@@ -706,12 +706,12 @@
     held, spec_held, sums_ref, in_sems, out_sems,
 ):
     moves = []
-    for part in range(8):
-        rows = pl.ds(8 * part, 8)
-        moves.append((out_hbm.at[rows], held.at[rows], output.at[rows]))
     for part in range(2):
         rows = pl.ds(8 * part, 8)
         moves.append((spec_hbm.at[rows], spec_held.at[rows], spec_out.at[rows]))
+    for part in range(16):
+        rows = pl.ds(4 * part, 4)
+        moves.append((out_hbm.at[rows], held.at[rows], output.at[rows]))
     ins = [
         pltpu.make_async_copy(source, middle, in_sems.at[at])
         for at, (source, middle, _) in enumerate(moves)
@@ -720,7 +720,7 @@
         pltpu.make_async_copy(middle, target, out_sems.at[at])
         for at, (_, middle, target) in enumerate(moves)
     ]
-    sums_copy = pltpu.make_async_copy(sums_hbm, sums_ref, in_sems.at[10])
+    sums_copy = pltpu.make_async_copy(sums_hbm, sums_ref, in_sems.at[18])
     for copy in ins:
         copy.start()
     sums_copy.start()
@@ -752,8 +752,8 @@
             pltpu.VMEM(out.shape, BF16),
             pltpu.VMEM(d_spec.shape, F32),
             pltpu.VMEM((8, 8, 128), F32),
-            pltpu.SemaphoreType.DMA((11,)),
-            pltpu.SemaphoreType.DMA((10,)),
+            pltpu.SemaphoreType.DMA((19,)),
+            pltpu.SemaphoreType.DMA((18,)),
         ],
         compiler_params=pltpu.CompilerParams(vmem_limit_bytes=58 * MIB),
     )(out, d_spec, sums)

time: 64.4 us -> 64.8 us (level)
  no operation moved by 1% of the time
where the time goes in v9:
time: 64.8 us; the launch traced here: 64.7 us
  Pallas kernels  63.9 us (99%)
  between operations  0.8 us (1%)
    pallas_call x1, Pallas kernels, layer_call(): pl.pallas_call(layer_kernel, out_shape=(jax.ShapeDtypeStruct(cells, BF16)...  58.8 us
    pallas_call x1, Pallas kernels, results_call(): pl.pallas_call(results_kernel, out_shape=(jax.ShapeDtypeStruct(out.shape,...  5.05 us

profile of v9, /device:TPU:1, one launch (start us, length us, event | category | flops | bytes accessed | tf_op | source)
XLA Modules:
  0.0 64.7 jit_solution(15809191693753447215)
XLA Ops:
  0.6 58.8 %shard_map.165 = (bf16[64,2,128,128]{3,2,1,0:T(8,128)(2,1)}, f32[16,64,128]{2,1,0:T(8,128)}, f32[8,8,128]{2,1,0:T(8,128)}) custom-call(bf16[64,2,128,128]{3,2,1,0:T(8,128)(2,1)} %field.1, bf16[64,2,128,128]{3,2,1,0:T(8,128)(2,1)} %bitcast.6, bf16[16,64,128]{2,1,0:T(8,128)(2,1)} %bitcast.7, bf16[64,64]{1,0:T(8,128)(2,1)} %wl_hbm.1, s32[30,64]{1,0:T(8,128)} %bitcast.8, ...), custom_call_target="tpu_custom_call" | custom-call | tf_op jit(solution)/shard_map/pallas_call | solution.py:645
  59.5 5.1 %shard_map.166 = (bf16[64,2,128,128]{3,2,1,0:T(8,128)(2,1)}, f32[16,64,128]{2,1,0:T(8,128)}, f32[64,64]{1,0:T(8,128)}, f32[1,64]{1,0:T(1,128)}) custom-call(bf16[64,2,128,128]{3,2,1,0:T(8,128)(2,1)} %get-tuple-element.11.out_hbm, f32[16,64,128]{2,1,0:T(8,128)} %get-tuple-element.12.spec_hbm, f32[8,8,128]{2,1,0:T(8,128)} %get-tuple-element.13.sums_hbm), custom_call_target="tpu_custom_call" | custom-call | tf_op jit(solution)/shard_map/pallas_call | solution.py:741
